TPU v7x, 512 devices: a whole 4x4x16 slice. The times are simulated.
512 devices in a mesh: sect: 32 (over z, y_lo), tp: 16 (over y_hi, x, core).
Axes of the slice: x: 4, y: 4 (y_hi: 2, y_lo: 2; y = y_hi * 2 + y_lo), z: 16, core: 2. Of those that a mesh axis runs over, the one named last changes fastest.
Arguments:
- hidden_pre: bfloat16 [16384, 8192], P('sect', 'tp'), may hold values from -30 to 30
- norm_gain: bfloat16 [8192], P('tp'), may hold values from 0.099609375 to 1.8984375
- kv_weight: bfloat16 [8192, 2048], P('tp'), may hold values from -0.0625 to 0.0625
- query_pre: bfloat16 [16384, 8192], P('sect', 'tp'), may hold values from -600 to 600
- doc_ids: int32 [32, 512], P('sect'), may hold values from 0 to 7, never falling along the last dimension, each value on 1 to 256 neighbouring positions
- page_dest: int32 [1024, 1], P('sect'), may hold values from 0 to 31, as said below
- old_pages: bfloat16 [512, 16, 16, 128], P('sect'), may hold values from -6 to 6
- query_dec: bfloat16 [512, 8192], P('sect', 'tp'), may hold values from -600 to 600
- page_table: int32 [512, 16], P('sect'), may hold values from 0 to 79, as said below
- ctx_len: int32 [512], P('sect'), may hold values from 1 to 256, as said below
Outputs:
- prefill_out: bfloat16 [16384, 8192], P('sect', 'tp')
- decode_out: bfloat16 [512, 8192], P('sect', 'tp')
Inputs may be any that keep to these rules, and one draw needn't show every extreme that they name: `page_dest`: of one section's pages at most 2 go to any one section, and in every section's pages some section receives exactly 2. `page_table`: the entries of a row are distinct; each names a slot below 16 or a slot 16 + s * 2 + c of the row's own section where c is below the number of pages that section s hands to it. `ctx_len`: in every section some row has the full context of 256 tokens.
All inputs are finite; a program needn't handle non-finite values.
Results may differ from a plain program's by a relative error of at most 0.012.
The roundings to bfloat16 on the way count: a program that leaves them out, or rounds other values in their place, can miss the bound.
Values may be sent and summed in bfloat16 or wider, within the bound.
A program may use at most 64 MiB of HBM per device.

v0:
```python
import jax
import jax.numpy as jnp
from jax import lax
from jax.sharding import PartitionSpec as P

D = 8192
HEADS = 64
KVH = 8
PAGE = 16


NORM_EPS = 1e-05


def softmax_rows(scores):
    row_peak = jnp.max(scores, axis=-1, keepdims=True)
    raised = jnp.exp(scores - row_peak)
    return raised / jnp.sum(raised, axis=-1, keepdims=True)


def attend_prefill(queries, key_part, value_part, doc_row, groups):
    tok_count = queries.shape[0]
    head_dim = key_part.shape[-1]
    query_heads = queries.reshape(tok_count, groups, -1, head_dim)
    scores = jnp.einsum(
        "tgnd,sgd->gnts", query_heads, key_part, preferred_element_type=jnp.float32
    ) * head_dim ** (-0.5)
    positions = jnp.arange(tok_count)
    allowed = (doc_row[:, None] == doc_row[None, :]) & (positions[None, :] <= positions[:, None])
    scores = jnp.where(allowed, scores, -jnp.inf)
    weights = softmax_rows(scores).astype(jnp.bfloat16)
    mixed = jnp.einsum("gnts,sgd->tgnd", weights, value_part, preferred_element_type=jnp.float32)
    return mixed.reshape(tok_count, -1).astype(jnp.bfloat16)


def local(
    hidden_pre,
    norm_gain,
    kv_weight,
    query_pre,
    doc_ids,
    page_dest,
    old_pages,
    query_dec,
    page_table,
    ctx_len,
):
    tp_count = lax.axis_size("tp")
    tp_index = lax.axis_index("tp")
    sect_count = lax.axis_size("sect")
    tok_count = hidden_pre.shape[0]
    head_dim = old_pages.shape[-1]
    kv_cols = kv_weight.shape[1]
    kv_heads = kv_cols // (2 * head_dim)
    groups = max(1, kv_heads // tp_count)
    group_cols = 2 * head_dim * groups
    first_group = tp_index * (query_pre.shape[1] // head_dim) // (HEADS // KVH)
    widened = hidden_pre.astype(jnp.float32)
    part_sq = jnp.sum(widened * widened, axis=1)
    scaled = (widened * norm_gain.astype(jnp.float32)).astype(jnp.bfloat16)
    total_sq = lax.psum(part_sq, "tp")
    share_rows = tok_count // tp_count
    term = jnp.dot(scaled, kv_weight, preferred_element_type=jnp.float32)
    summed = lax.psum_scatter(term, "tp", scatter_dimension=0, tiled=True)
    share_sq = lax.dynamic_slice_in_dim(total_sq, tp_index * share_rows, share_rows, 0)
    kv_share = (summed * lax.rsqrt(share_sq / D + NORM_EPS)[:, None]).astype(jnp.bfloat16)
    gathered = lax.all_gather(kv_share, "tp", axis=0, tiled=True)
    head_kv = lax.dynamic_slice_in_dim(gathered, first_group * 2 * head_dim, group_cols, 1)
    kv_pairs = head_kv.reshape(tok_count, groups, 2, head_dim)
    prefill_out = attend_prefill(
        query_pre, kv_pairs[:, :, 0], kv_pairs[:, :, 1], doc_ids[0], groups
    )
    page_count = tok_count // PAGE
    slot_cap = max(2, 2 * page_count // sect_count)
    pay_width = head_kv.shape[1]
    page_target = page_dest[:, 0]
    page_order = jnp.arange(page_count)
    earlier = (page_target[None, :] == page_target[:, None]) & (
        page_order[None, :] < page_order[:, None]
    )
    send_slot = page_target * slot_cap + jnp.sum(earlier, axis=1)
    chooser = (jnp.arange(sect_count * slot_cap)[:, None] == send_slot[None, :]).astype(
        jnp.bfloat16
    )
    outgoing = jnp.dot(
        chooser, head_kv.reshape(page_count, PAGE * pay_width), preferred_element_type=jnp.float32
    ).astype(jnp.bfloat16)
    arrived = lax.all_to_all(
        outgoing.reshape(sect_count, slot_cap * PAGE * pay_width),
        "sect",
        split_axis=0,
        concat_axis=0,
        tiled=True,
    )
    arrived = arrived.reshape(sect_count * slot_cap, PAGE, pay_width)
    resident = lax.dynamic_slice_in_dim(old_pages, first_group * 2, 2 * groups, 2)
    resident = resident.reshape(old_pages.shape[0], PAGE, group_cols)
    page_pool = jnp.concatenate([resident, arrived], axis=0)
    row_count = query_dec.shape[0]
    picked = page_pool[page_table]
    ctx_count = picked.shape[1] * PAGE
    picked = picked.reshape(row_count, ctx_count, groups, 2, head_dim)
    query_heads = query_dec.reshape(row_count, groups, -1, head_dim)
    scores = jnp.einsum(
        "rgnd,rcgd->rgnc", query_heads, picked[:, :, :, 0], preferred_element_type=jnp.float32
    ) * head_dim ** (-0.5)
    live_mask = jnp.arange(ctx_count)[None, :] < ctx_len[:, None]
    scores = jnp.where(live_mask[:, None, None, :], scores, -jnp.inf)
    weights = softmax_rows(scores).astype(jnp.bfloat16)
    mixed = jnp.einsum(
        "rgnc,rcgd->rgnd", weights, picked[:, :, :, 1], preferred_element_type=jnp.float32
    )
    decode_out = mixed.reshape(row_count, -1).astype(jnp.bfloat16)
    return (prefill_out, decode_out)


def solution(mesh):
    in_specs = (
        P("sect", "tp"),
        P("tp"),
        P("tp", None),
        P("sect", "tp"),
        P("sect", None),
        P("sect", None),
        P("sect", None, None, None),
        P("sect", "tp"),
        P("sect", None),
        P("sect"),
    )
    out_specs = (P("sect", "tp"), P("sect", "tp"))
    return jax.shard_map(local, mesh=mesh, in_specs=in_specs, out_specs=out_specs, check_vma=False)
```

profile of v0, /device:TPU:1, one launch (start us, length us, event | category | flops | bytes accessed | tf_op | source)
XLA Modules:
  0.0 277.7 jit_solution(6590693970543760219)
XLA Ops:
  7.2 0.8 convert_element_type.45
  8.0 0.7 copy-done
  8.8 4.3 %fusion.16 = f32[512,2048]{1,0:T(8,128)} fusion(bf16[512,2048]{1,0:T(8,128)(2,1)S(1)} %copy-done, bf16[512,512]{1,0:T(8,128)(2,1)} %param.10, f32[512]{0:T(512)S(1)} %convert_element_type.45), kind=kOutput, calls=%fused_computation.27 | convolution fusion | flops 1074528256 | bytes 6817792 | tf_op jit(solution)/shard_map/dot_general | solution.py:63
  13.4 39.4 %psum.7 = f32[512]{0:T(512)S(1)} all-reduce(f32[512]{0:T(512)S(1)} %fusion.14), channel_id=1, replica_groups=mesh['sect'=32,'tp'=16] {'tp'}, use_global_device_ids=true, to_apply=%region_2.3 | all-reduce | flops 512 | bytes 4096 | tf_op jit(solution)/shard_map/psum | solution.py:61
  52.8 67.8 %reduce-scatter.2.cloned.1.call-done = f32[32,2048]{1,0:T(8,128)} async-done(((f32[512,2048]{1,0:T(8,128)}), f32[32,2048]{1,0:T(8,128)}) %reduce-scatter.2.cloned.1.call-update) | async-done | bytes 262160 | tf_op jit(solution)/shard_map/reduce_scatter | solution.py:64
  120.7 1.7 multiply_convert_fusion
  122.4 1.2 constant_dynamic-slice_fusion
  123.8 0.6 reshape.134
  124.6 65.1 %all-gather.2.cloned.1.call-done = bf16[512,2048]{1,0:T(8,128)(2,1)} async-done(((bf16[32,2048]{1,0:T(8,128)(2,1)}), bf16[512,2048]{1,0:T(8,128)(2,1)}) %all-gather.2.cloned.1.call-update) | async-done | bytes 2097168 | tf_op jit(solution)/shard_map/all_gather | solution.py:67
  189.7 1.0 constant_dynamic-slice_fusion.1
  190.8 1.1 convolution_convert_fusion
  191.9 2.5 all_to_all.8
  194.4 0.6 broadcast.45
  195.0 4.6 %reduce.7 = bf16[32,8192]{1,0:T(8,128)(2,1)} reduce(bf16[32,1,8192]{2,1,0:T(2,128)(2,1)S(1)} %all_to_all.8, bf16[]{:T(256)} %broadcast.45), dimensions={1}, to_apply=%all_to_all.8.reduce_sub_computation | reduce | bytes 1048578 | tf_op jit(solution)/shard_map/all_to_all | solution.py:88
  199.6 2.2 reshape.150
  201.9 12.6 %all-to-all-start = ((bf16[32,2,4096]{2,1,0:T(2,128)(2,1)}), bf16[32,2,4096]{2,1,0:T(2,128)(2,1)}, u32[]{:S(2)}, u32[]{:S(2)}) async-start(bf16[32,2,4096]{2,1,0:T(2,128)(2,1)} %reshape.150), calls=%async_computation.1 | async-start | bytes 1048576 | tf_op jit(solution)/shard_map/all_to_all | solution.py:88
  214.6 0.2 fusion.15
  215.0 1.9 fusion.2
  216.9 0.9 fusion.1
  217.8 1.5 fusion.6
  219.3 1.0 copy.46
  220.3 26.1 %all-to-all-done = bf16[32,2,4096]{2,1,0:T(2,128)(2,1)} async-done(((bf16[32,2,4096]{2,1,0:T(2,128)(2,1)}), bf16[32,2,4096]{2,1,0:T(2,128)(2,1)}, u32[]{:S(2)}, u32[]{:S(2)}) %all-to-all-start) | async-done | bytes 524320 | tf_op jit(solution)/shard_map/all_to_all | solution.py:88
  246.4 3.6 %reshape.151 = bf16[32,1,8192]{2,1,0:T(2,128)(2,1)S(1)} reshape(bf16[32,2,4096]{2,1,0:T(2,128)(2,1)} %all-to-all-done) | data formatting | bytes 1048576
  250.0 4.0 %reduce.6 = bf16[32,8192]{1,0:T(8,128)(2,1)} reduce(bf16[32,1,8192]{2,1,0:T(2,128)(2,1)S(1)} %reshape.151, bf16[]{:T(256)} %constant.57), dimensions={1}, to_apply=%all_to_all.7.reduce_sub_computation | reduce | bytes 1048578 | tf_op jit(solution)/shard_map/all_to_all | solution.py:88
  254.0 1.3 reshape.131
  255.3 2.0 gather_fusion
  257.4 4.0 %reshape.132 = bf16[16,256,1,2,128]{4,3,1,0,2:T(2,128)(2,1)} reshape(bf16[256,16,256]{2,1,0:T(8,128)(2,1)} %gather_fusion) | data formatting | bytes 4194304 | tf_op jit(solution)/shard_map/reshape | solution.py:102
  261.3 6.4 %fusion.27 = (bf16[16,256,1,1,128]{4,3,1,0,2:T(2,128)(2,1)S(1)}, bf16[16,256,1,1,128]{4,3,1,0,2:T(2,128)(2,1)}) fusion(bf16[16,256,1,2,128]{4,3,1,0,2:T(2,128)(2,1)} %reshape.132), kind=kLoop, calls=%fused_computation.52 | loop fusion | bytes 4194304 | tf_op jit(solution)/shard_map/slice | solution.py:105
  267.8 0.4 fusion.12
  268.2 0.2 fusion.28
  268.3 1.9 convolution_convert_fusion.1
  270.3 0.6 copy.64
  (31 shorter events, 1.2 us)
Async XLA Ops:
  7.2 1.6 copy-start
  7.2 113.5 %reduce-scatter.2.cloned.1.call-start = ((), (), s32[]{:S(2)}) async-start(), calls=%async_computation.2 | async-start | bytes 4456448 | tf_op jit(solution)/shard_map/reduce_scatter | solution.py:64
  8.8 4.4 %copy-start.1 = (bf16[512,512]{1,0:T(8,128)(2,1)S(1)}, bf16[512,512]{1,0:T(8,128)(2,1)}, u32[]{:S(2)}) copy-start(bf16[512,512]{1,0:T(8,128)(2,1)} %param.10) | copy-start | bytes 1572868
  13.1 110.6 %copy-start.5 = (s32[16,16]{1,0:T(8,128)S(1)}, s32[16,16]{1,0:T(8,128)}, u32[]{:S(2)}) copy-start(s32[16,16]{1,0:T(8,128)} %param.18) | copy-start | bytes 3076
  13.1 110.7 %copy-start.2 = (bf16[16,512]{1,0:T(8,128)(2,1)S(1)}, bf16[16,512]{1,0:T(8,128)(2,1)}, u32[]{:S(2)}) copy-start(bf16[16,512]{1,0:T(8,128)(2,1)} %param.17) | copy-start | bytes 49156
  13.1 111.3 %copy-start.7 = (s32[32,1]{0,1:T(1,128)S(1)}, s32[32,1]{0,1:T(1,128)}, u32[]{:S(2)}) copy-start(s32[32,1]{0,1:T(1,128)} %param.15) | copy-start | bytes 388
  13.1 176.6 %all-gather.2.cloned.1.call-start = ((), (), s32[]{:S(2)}) async-start(), calls=%async_computation.3 | async-start | bytes 2228224 | tf_op jit(solution)/shard_map/all_gather | solution.py:67
  13.3 201.2 %copy-start.6 = (s32[16]{0:T(128)S(1)}, s32[16]{0:T(128)}, u32[]{:S(2)}) copy-start(s32[16]{0:T(128)} %param.19) | copy-start | bytes 196
  13.4 201.2 %copy-start.4 = (s32[1,512]{1,0:T(1,128)S(1)}, s32[1,512]{1,0:T(1,128)}, u32[]{:S(2)}) copy-start(s32[1,512]{1,0:T(1,128)} %param.14) | copy-start | bytes 6148
  201.9 44.5 %all-to-all-start = ((bf16[32,2,4096]{2,1,0:T(2,128)(2,1)}), bf16[32,2,4096]{2,1,0:T(2,128)(2,1)}, u32[]{:S(2)}, u32[]{:S(2)}) async-start(bf16[32,2,4096]{2,1,0:T(2,128)(2,1)} %reshape.150), calls=%async_computation.1 | async-start | bytes 1048576 | tf_op jit(solution)/shard_map/all_to_all | solution.py:88
  261.3 6.4 %copy-start.3 = (bf16[16,4,128]{2,1,0:T(4,128)(2,1)S(1)}, bf16[16,4,128]{2,1,0:T(4,128)(2,1)}, u32[]{:S(2)}) copy-start(bf16[16,4,128]{2,1,0:T(4,128)(2,1)} %reshape.134) | copy-start | bytes 49156
Sparse Core Ops, SparseCore 0:
  13.2 107.4 reduce-scatter.1
  125.1 64.5 all-gather.1
where the time goes:
time: 279 us; the launch traced here: 278 us
  waiting for transfers between devices  159 us (57%)
  blocking collectives  39.4 us (14%)
  local copies, waits for them, and re-layouts  28.3 us (10%)
  between operations  14.2 us (5%)
  other arithmetic  13 us (5%)
  starting transfers between devices  12.7 us (5%)
  matrix products  11.1 us (4%)
    reduce_scatter x1, waiting for transfers between devices, local(): summed = lax.psum_scatter(term, 'tp', scatter_dimension=0, tiled=True)  67.8 us
    all_gather x1, waiting for transfers between devices, local(): gathered = lax.all_gather(kv_share, 'tp', axis=0, tiled=True)  65.1 us
    psum x1, blocking collectives, local(): total_sq = lax.psum(part_sq, 'tp')  39.4 us
    all_to_all x1, waiting for transfers between devices, local(): lax.all_to_all(outgoing.reshape(sect_count, slot_cap * PAGE * pay_width),...  26.1 us
    all_to_all x1, starting transfers between devices, local(): lax.all_to_all(outgoing.reshape(sect_count, slot_cap * PAGE * pay_width),...  12.6 us
    all_to_all x2, other arithmetic, local(): lax.all_to_all(outgoing.reshape(sect_count, slot_cap * PAGE * pay_width),...  8.6 us
    unnamed x20, local copies, waits for them, and re-layouts  8.26 us
    slice x1, local copies, waits for them, and re-layouts, local(): picked[:, :, :, 0]  6.44 us
  transfers between devices with their start and end apart: 3, of which 3 were waited for; matrix products, arithmetic and copies ran while one was open for 3% of the time, Pallas kernels for 0%

commit v1 on v0

v1 whole, which is shorter than its diff:
```python
import jax
import jax.numpy as jnp
from jax import lax
from jax.sharding import PartitionSpec as P
import jax.experimental.pallas as pl
import jax.experimental.pallas.tpu as pltpu

D = 8192
HD = 128
PAGE = 16
TOK = 512
FEAT = 512
CHIPS = 8
SECT = 32
SLOTS = 2
MSG = SLOTS * PAGE
FRESH = SECT * MSG
ROWS = 16
NH = 4
OLD = 256
MAXP = 16
NORM_EPS = 1e-05
SCALE = HD ** -0.5
MESH = pl.DeviceIdType.MESH
F32 = jnp.float32
BF16 = jnp.bfloat16
RING = ((1, 2), (1, 1), (1, 3), (0, 2), (1, 0), (0, 1), (0, 3))
NEG = -jnp.inf
TINY = 1e-30
STEPS = 32000.0
VMEM_LIMIT = 60 * 2**20


def dot(a, b):
    return lax.dot_general(a, b, (((1,), (0,)), ((), ())), preferred_element_type=F32)


def dot_t(a, b):
    return lax.dot_general(a, b, (((1,), (1,)), ((), ())), preferred_element_type=F32)


def softmax_weights(scores):
    peak = jnp.max(scores, axis=-1, keepdims=True)
    raised = jnp.exp(scores - peak)
    return (raised * (1.0 / jnp.sum(raised, axis=-1, keepdims=True))).astype(BF16)


def kernel(
    hid, gain, weight, qpre, doc, pdest, oldp, qdec, table, ctx,
    o_pre, o_dec,
    hraw, graw, wv, docv, pdv, tabv, ctxs, hs, st, part, sibp, sbuf, rs, sstat, rstat, chooser, outg, kvh, pool,
    oldbuf, oldkv, qp, qd, pos, obuf, dbuf,
    in_sem, w_sem, sib_s, sib_r, ps_s, ps_r, rs_s, rs_r, sq_s, sq_r, aa_s, aa_r, out_sem, flood,
):
    s = lax.axis_index("sect")
    t = lax.axis_index("tp")
    k = t % 2
    x = (t // 2) % 4
    yh = t // 8
    g = t // 2
    z = s // 2
    yl = s % 2
    sib = (s, t + 1 - 2 * k)

    def ring_dst(i):
        dy, dx = RING[i]
        return ((yh + dy) % 2) * 4 + (x + dx) % 4

    def ring_src(i):
        dy, dx = RING[i]
        return ((yh + dy) % 2) * 4 + (x + 4 - dx) % 4

    def sect_peer(i):
        j = i // 2
        sign = 1 - 2 * (j % 2)
        dz = 8 + sign * ((j + 1) // 2)
        yx = 1 - i % 2
        return dz, yx

    def z_peer(dz, yx):
        return (((z + dz + 16) % 16) * 2 + (yl + yx) % 2, t)

    def remote(src, dst, ss, rr, dev):
        c = pltpu.make_async_remote_copy(
            src_ref=src, dst_ref=dst, send_sem=ss, recv_sem=rr, device_id=dev, device_id_type=MESH
        )
        c.start()
        return c

    def load(src, dst, sem):
        c = pltpu.make_async_copy(src, dst, sem)
        c.start()
        return c

    bar = pltpu.get_barrier_semaphore()
    greeted = [sib] + [(s, ring_dst(i) * 2 + k) for i in range(7)]
    greeted += [z_peer(1, 0), z_peer(-1, 0), z_peer(1, 1), z_peer(-1, 1), z_peer(0, 1)]
    for peer in greeted:
        pl.semaphore_signal(bar, inc=1, device_id=peer, device_id_type=MESH)

    order = [ring_dst(i) for i in range(7)] + [g]
    c_hid = load(hid, hraw, in_sem.at[0])
    c_gain = load(gain, graw, in_sem.at[1])
    c_w = [
        load(
            weight.at[:, pl.ds(pl.multiple_of(j * 2 * HD, 2 * HD), 2 * HD)], wv.at[j], w_sem.at[n]
        )
        for n, j in enumerate(order)
    ]
    c_pd = load(pdest, pdv, in_sem.at[2])
    c_doc = load(doc, docv, in_sem.at[3])
    c_tab = load(table, tabv, in_sem.at[4])
    c_ctx = load(ctx, ctxs, in_sem.at[5])
    c_old = load(oldp, oldbuf, in_sem.at[6])
    c_qp = load(qpre, qp, in_sem.at[7])
    c_qd = load(qdec, qd, in_sem.at[8])

    c_hid.wait()
    c_gain.wait()
    h = hraw[...].astype(F32)
    hs[...] = (h * graw[...].astype(F32).reshape(1, FEAT)).astype(BF16)
    hh = h * h
    folded = hh[:, 0:128] + hh[:, 128:256] + hh[:, 256:384] + hh[:, 384:512]
    st[k] = jnp.broadcast_to(jnp.sum(folded.T, axis=0, keepdims=True), (8, TOK))
    for n, j in enumerate(order):
        c_w[n].wait()
        both = dot(hs[...], wv[j])
        part[j, 0] = both[:, :HD]
        part[j, 1] = both[:, HD:]

    pl.semaphore_wait(bar, len(greeted))

    c_st = remote(st.at[k], st.at[k], sib_s.at[0], sib_r.at[0], sib)
    c_ps = [
        remote(part.at[j, 1 - k], sibp.at[j], ps_s.at[n], ps_r.at[n], sib) for n, j in enumerate(order)
    ]
    c_st.wait_recv()
    chip_sq = st[0] + st[1]
    chip_ms = chip_sq * (1.0 / (2 * FEAT)) + TINY
    row_mul = lax.rsqrt(chip_ms).T[:, 0:1]
    sstat[g, :, 0:TOK] = chip_sq
    c_rs, c_sq = [], []
    for n, j in enumerate(order):
        c_ps[n].wait_recv()
        total = part[j, k] + sibp[j]
        if n < 7:
            level = total * row_mul
            top = jnp.maximum(jnp.max(jnp.abs(level), axis=0, keepdims=True), TINY)
            sbuf[j] = jnp.round(level * (STEPS / top)).astype(jnp.int32).astype(jnp.int16)
            sstat[j, :, 0:TOK] = chip_sq
            sstat[j, :, TOK:] = jnp.broadcast_to(top * (1.0 / STEPS), (8, HD))
            peer = (s, j * 2 + k)
            c_sq.append(remote(sstat.at[j], rstat.at[g], sq_s.at[n], sq_r.at[n], peer))
            c_rs.append(remote(sbuf.at[j], rs.at[g], rs_s.at[n], rs_r.at[n], peer))
        else:
            part[j, k] = total

    def flood_round(r):
        for sign in (1, -1):
            pl.semaphore_signal(
                flood.at[r], inc=1, device_id=z_peer(sign * (1 << r), 0), device_id_type=MESH
            )
        pl.semaphore_wait(flood.at[r], 2)

    flood_round(0)

    c_pd.wait()
    eye = lax.broadcasted_iota(jnp.int32, (32, 32), 0) == lax.broadcasted_iota(jnp.int32, (32, 32), 1)
    page_col = jnp.sum(jnp.where(eye, jnp.broadcast_to(pdv[...], (32, 32)), 0), axis=1, keepdims=True)
    page_of = lax.broadcasted_iota(jnp.int32, (32, TOK), 1) // PAGE
    page_row = lax.broadcasted_iota(jnp.int32, (32, TOK), 0)
    page_b = jnp.broadcast_to(page_col, (32, TOK))
    dest_tok = jnp.sum(jnp.where(page_of == page_row, page_b, 0), axis=0, keepdims=True)
    rank_tok = jnp.sum(
        jnp.where((page_b == dest_tok) & (page_row < page_of), 1, 0), axis=0, keepdims=True
    )
    tok_in = lax.broadcasted_iota(jnp.int32, (1, TOK), 1) % PAGE
    target = (dest_tok * SLOTS + rank_tok) * PAGE + tok_in
    for c in range(FRESH // 128):
        rows = lax.broadcasted_iota(jnp.int32, (128, TOK), 0) + c * 128
        chooser[c * 128:(c + 1) * 128, :] = jnp.where(rows == target, 1.0, 0.0).astype(BF16)

    flood_round(1)

    c_old.wait()
    for c in range(OLD // 32):
        blk = oldbuf[2 * c:2 * c + 2].reshape(32, 16, HD).astype(F32)
        head = lax.broadcasted_iota(jnp.int32, (1, 16, 1), 1)
        for m in range(2):
            one = jnp.sum(jnp.where(head == 2 * g + m, blk, 0.0), axis=1)
            oldkv[m, c * 32:(c + 1) * 32, :] = one.astype(BF16)

    c_tab.wait()
    c_ctx.wait()
    col = lax.broadcasted_iota(jnp.int32, (ROWS, OLD + FRESH), 1)
    col_slot = col // PAGE
    col_in = col % PAGE
    where_pos = jnp.full((ROWS, OLD + FRESH), 1 << 20, jnp.int32)
    tab = tabv[...]
    for j in range(MAXP):
        where_pos = jnp.where(tab[:, j:j + 1] == col_slot, j * PAGE + col_in, where_pos)
    row_id = lax.broadcasted_iota(jnp.int32, (ROWS, 1), 0)
    lens = jnp.zeros((ROWS, 1), jnp.int32)
    for r in range(ROWS):
        lens = jnp.where(row_id == r, ctxs[r], lens)
    pos[...] = jnp.where(where_pos < lens, 0.0, NEG)

    flood_round(2)

    summed = part[g, k]
    total_sq = chip_sq
    for i in (5, 6, 3, 4, 1, 2, 0):
        c_sq[i].wait_recv()
        src = ring_src(i)
        other_sq = rstat[src, :, 0:TOK]
        total_sq = total_sq + other_sq
        other_ms = other_sq * (1.0 / (2 * FEAT)) + TINY
        row_scale = (other_ms * lax.rsqrt(other_ms)).T[:, 0:1]
        col_scale = rstat[src, 0:1, TOK:]
        c_rs[i].wait_recv()
        summed = summed + rs[src].astype(jnp.int32).astype(F32) * col_scale * row_scale
    inv = lax.rsqrt(total_sq / D + NORM_EPS).T[:, 0:1]
    kvh[k] = (summed * inv).astype(BF16)
    c_kv = remote(kvh.at[k], kvh.at[k], sib_s.at[1], sib_r.at[1], sib)

    for c in range(4):
        outg[c * 256:(c + 1) * 256, :] = dot(chooser[c * 256:(c + 1) * 256, :], kvh[k]).astype(BF16)

    def page_copy(i):
        dz, yx = sect_peer(i)
        dst = ((z + dz) % 16) * 2 + (yl + yx) % 2
        return pltpu.make_async_remote_copy(
            src_ref=outg.at[pl.ds(pl.multiple_of(dst * MSG, MSG), MSG)],
            dst_ref=pool.at[k, pl.ds(pl.multiple_of(s * MSG, MSG), MSG)],
            send_sem=aa_s.at[i], recv_sem=aa_r.at[i], device_id=(dst, t), device_id_type=MESH,
        )

    def page_start(i, _):
        page_copy(i).start()
        return 0

    lax.fori_loop(0, 31, page_start, 0)
    own = pl.ds(pl.multiple_of(s * MSG, MSG), MSG)
    pool[k, own, :] = outg[own, :]

    c_qp.wait()
    c_doc.wait()
    doc_row = docv[...].astype(F32)
    doc_col = jnp.broadcast_to(doc_row, (8, TOK)).T[:, 0:1]
    c_kv.wait_recv()
    out_copies = []
    for b in range(4):
        lo, hi = max(0, b - 2) * 128, (b + 1) * 128
        q0 = b * 128
        tq = lax.broadcasted_iota(jnp.int32, (128, hi - lo), 0) + q0
        tk = lax.broadcasted_iota(jnp.int32, (128, hi - lo), 1) + lo
        allowed = (doc_col[q0:hi, :] == doc_row[:, lo:hi]) & (tk <= tq)
        keys = kvh[0, lo:hi, :]
        values = kvh[1, lo:hi, :]
        for n in range(NH):
            sc = dot_t(qp[q0:hi, n * HD:(n + 1) * HD], keys) * SCALE
            wts = softmax_weights(jnp.where(allowed, sc, NEG))
            obuf[q0:hi, n * HD:(n + 1) * HD] = dot(wts, values).astype(BF16)
        out_copies.append(load(obuf.at[q0:hi], o_pre.at[q0:hi], out_sem.at[b]))

    c_qd.wait()
    qs = jnp.concatenate([qd[:, n * HD:(n + 1) * HD] for n in range(NH)], axis=0)
    sc_old = dot_t(qs, oldkv[0]) * SCALE
    mask = pos[...]
    mask = jnp.concatenate([mask] * NH, axis=0)
    sc_old = sc_old + mask[:, :OLD]
    peak_old = jnp.max(sc_old, axis=-1, keepdims=True)

    def page_wait(i, _):
        page_copy(i).wait_recv()
        return 0

    lax.fori_loop(0, 31, page_wait, 0)
    c_pool = remote(pool.at[k], pool.at[k], sib_s.at[2], sib_r.at[2], sib)
    c_pool.wait_recv()
    sc_new = dot_t(qs, pool[0]) * SCALE + mask[:, OLD:]
    peak = jnp.maximum(peak_old, jnp.max(sc_new, axis=-1, keepdims=True))
    e_old = jnp.exp(sc_old - peak)
    e_new = jnp.exp(sc_new - peak)
    norm = 1.0 / (jnp.sum(e_old, axis=-1, keepdims=True) + jnp.sum(e_new, axis=-1, keepdims=True))
    mixed = dot((e_old * norm).astype(BF16), oldkv[1]) + dot((e_new * norm).astype(BF16), pool[1])
    mixed = mixed.astype(BF16)
    for n in range(NH):
        dbuf[:, n * HD:(n + 1) * HD] = mixed[n * ROWS:(n + 1) * ROWS]
    out_copies.append(load(dbuf, o_dec, out_sem.at[4]))

    for c in [c_st, c_kv, c_pool] + c_ps + c_rs + c_sq:
        c.wait_send()

    def page_sent(i, _):
        page_copy(i).wait_send()
        return 0

    lax.fori_loop(0, 31, page_sent, 0)
    for c in out_copies:
        c.wait()


def local(hidden_pre, norm_gain, kv_weight, query_pre, doc_ids, page_dest, old_pages, query_dec, page_table, ctx_len):
    any_spec = pl.BlockSpec(memory_space=pl.ANY)
    dma = pltpu.SemaphoreType.DMA
    vm = pltpu.VMEM
    I32 = jnp.int32
    return pl.pallas_call(
        kernel,
        name="serve",
        out_shape=(
            jax.ShapeDtypeStruct((TOK, NH * HD), BF16),
            jax.ShapeDtypeStruct((ROWS, NH * HD), BF16),
        ),
        in_specs=[any_spec] * 10,
        out_specs=(any_spec, any_spec),
        scratch_shapes=[
            vm((TOK, FEAT), BF16), vm((FEAT,), BF16), vm((CHIPS, FEAT, 2 * HD), BF16),
            vm((1, TOK), I32), vm((1, 32), I32), vm((ROWS, MAXP), I32), pltpu.SMEM((ROWS,), I32),
            vm((TOK, FEAT), BF16), vm((2, 8, TOK), F32),
            vm((CHIPS, 2, TOK, HD), F32), vm((CHIPS, TOK, HD), F32),
            vm((CHIPS, TOK, HD), jnp.int16), vm((CHIPS, TOK, HD), jnp.int16),
            vm((CHIPS, 8, TOK + HD), F32), vm((CHIPS, 8, TOK + HD), F32),
            vm((FRESH, TOK), BF16), vm((FRESH, HD), BF16), vm((2, TOK, HD), BF16), vm((2, FRESH, HD), BF16),
            vm((16, 16, 16, HD), BF16), vm((2, OLD, HD), BF16), vm((TOK, NH * HD), BF16),
            vm((ROWS, NH * HD), BF16), vm((ROWS, OLD + FRESH), F32),
            vm((TOK, NH * HD), BF16), vm((ROWS, NH * HD), BF16),
            dma((9,)), dma((8,)), dma((3,)), dma((3,)), dma((8,)), dma((8,)), dma((7,)), dma((7,)),
            dma((7,)), dma((7,)), dma((31,)), dma((31,)), dma((5,)), pltpu.SemaphoreType.REGULAR((3,)),
        ],
        compiler_params=pltpu.CompilerParams(
            collective_id=0, has_side_effects=True, vmem_limit_bytes=VMEM_LIMIT
        ),
    )(
        hidden_pre, norm_gain, kv_weight, query_pre, doc_ids, page_dest.reshape(1, 32), old_pages,
        query_dec, page_table, ctx_len,
    )


def solution(mesh):
    in_specs = (
        P("sect", "tp"),
        P("tp"),
        P("tp", None),
        P("sect", "tp"),
        P("sect", None),
        P("sect", None),
        P("sect", None, None, None),
        P("sect", "tp"),
        P("sect", None),
        P("sect"),
    )
    out_specs = (P("sect", "tp"), P("sect", "tp"))
    return jax.shard_map(local, mesh=mesh, in_specs=in_specs, out_specs=out_specs, check_vma=False)
```

time: 279 us -> 60.5 us (0.22)
  waiting for transfers between devices: 159 us -> 0 us
  Pallas kernels: 0 us -> 56.4 us
  blocking collectives: 39.4 us -> 0 us
  local copies, waits for them, and re-layouts: 28.3 us -> 3.19 us
  between operations: 14.2 us -> 0.64 us
  other arithmetic: 13 us -> 0 us
  starting transfers between devices: 12.7 us -> 0 us
  matrix products: 11.1 us -> 0 us
    reduce_scatter x1 -> x0, waiting for transfers between devices: 67.8 us -> none  [local(): summed = lax.psum_scatter(term, 'tp', scatter_dimension=0, tiled=True)]
    all_gather x1 -> x0, waiting for transfers between devices: 65.1 us -> none  [local(): gathered = lax.all_gather(kv_share, 'tp', axis=0, tiled=True)]
    pallas_call x0 -> x1, Pallas kernels: none -> 56.4 us  [local(): pl.pallas_call(kernel, name='serve', out_shape=(jax.ShapeDtypeStruct((TOK...]
    psum x1 -> x0, blocking collectives: 39.4 us -> none  [local(): total_sq = lax.psum(part_sq, 'tp')]
    all_to_all x1 -> x0, waiting for transfers between devices: 26.1 us -> none  [local(): lax.all_to_all(outgoing.reshape(sect_count, slot_cap * PAGE * pay_width),...]
    all_to_all x1 -> x0, starting transfers between devices: 12.6 us -> none  [local(): lax.all_to_all(outgoing.reshape(sect_count, slot_cap * PAGE * pay_width),...]
    dot_general x6 -> x0, matrix products: 11.1 us -> none  [the longest x1 4.3 us: local(): term = jnp.dot(scaled, kv_weight, preferred_element_type=jnp.float32)]
    all_to_all x2 -> x0, other arithmetic: 8.6 us -> none  [local(): lax.all_to_all(outgoing.reshape(sect_count, slot_cap * PAGE * pay_width),...]
  transfers between devices with their start and end apart: 3 -> 0, of which waited for: 3 -> 0; matrix products, arithmetic and copies ran while one was open for 3% -> 0% of each run, Pallas kernels for 0% -> 0%
where the time goes in v1:
time: 60.5 us; the launch traced here: 60.3 us
  Pallas kernels  56.4 us (93%)
  local copies, waits for them, and re-layouts  3.19 us (5%)
  between operations  0.64 us (1%)
    pallas_call x1, Pallas kernels, local(): pl.pallas_call(kernel, name='serve', out_shape=(jax.ShapeDtypeStruct((TOK...  56.4 us
    unnamed x2, local copies, waits for them, and re-layouts  3.19 us

profile of v1, /device:TPU:1, one launch (start us, length us, event | category | flops | bytes accessed | tf_op | source)
XLA Modules:
  0.0 60.3 jit_solution(5526948128546699945)
XLA Ops:
  0.6 56.4 %serve.1 = (bf16[512,512]{1,0:T(8,128)(2,1)}, bf16[16,512]{1,0:T(8,128)(2,1)}) custom-call(bf16[512,512]{1,0:T(8,128)(2,1)} %hid.1, bf16[512]{0:T(512)(128)(2,1)} %gain.1, bf16[512,2048]{1,0:T(8,128)(2,1)} %weight.1, bf16[512,512]{1,0:T(8,128)(2,1)} %qpre.1, s32[1,512]{1,0:T(1,128)} %doc.1, s32[1,32]{1,0:T(1,128)} %bitcast.1, ...), custom_call_target="tpu_custom_call" | custom-call | tf_op jit(solution)/shard_map/serve/pallas_call | solution.py:309
  57.1 1.9 %copy.14 = bf16[512,512]{1,0:T(8,128)(2,1)} copy(bf16[512,512]{1,0:T(8,128)(2,1)} %get-tuple-element.4) | data formatting | bytes 1048576
  58.9 1.3 %copy.15 = bf16[16,512]{1,0:T(8,128)(2,1)} copy(bf16[16,512]{1,0:T(8,128)(2,1)} %get-tuple-element.5) | data formatting | bytes 32768

commit v2 on v1

v2 whole, which is shorter than its diff:
```python
import jax
import jax.numpy as jnp
from jax import lax
from jax.sharding import PartitionSpec as P
import jax.experimental.pallas as pl
import jax.experimental.pallas.tpu as pltpu

D = 8192
HD = 128
PAGE = 16
TOK = 512
FEAT = 512
CHIPS = 8
SECT = 32
SLOTS = 2
HALF = PAGE // 2
CH = TOK // 2
MSG = SLOTS * HALF
FRESH = SECT * SLOTS * PAGE
LAG = 3
ROWS = 16
NH = 4
OLD = 256
MAXP = 16
NORM_EPS = 1e-05
SCALE = HD ** -0.5
MESH = pl.DeviceIdType.MESH
F32 = jnp.float32
BF16 = jnp.bfloat16
RING = ((1, 2), (1, 1), (1, 3), (0, 2), (1, 0), (0, 1), (0, 3))
NEG = -jnp.inf
TINY = 1e-30
STEPS = 32000.0
VMEM_LIMIT = 60 * 2**20


def dot(a, b):
    return lax.dot_general(a, b, (((1,), (0,)), ((), ())), preferred_element_type=F32)


def dot_t(a, b):
    return lax.dot_general(a, b, (((1,), (1,)), ((), ())), preferred_element_type=F32)


def softmax_weights(scores):
    peak = jnp.max(scores, axis=-1, keepdims=True)
    raised = jnp.exp(scores - peak)
    return (raised * (1.0 / jnp.sum(raised, axis=-1, keepdims=True))).astype(BF16)


def kernel(
    hid, gain, weight, qpre, doc, pdest, oldp, qdec, table, ctx,
    o_pre, o_dec,
    hraw, graw, wv, docv, pdv, tabv, ctxs, hs, st, part, sibp, sbuf, rs, sstat, rstat, chooser, kvc, outg, kvh, pool,
    oldbuf, oldkv, qp, qd, pos, obuf, dbuf,
    in_sem, w_sem, sib_s, sib_r, ps_s, ps_r, rs_s, rs_r, sq_s, sq_r, aa_s, aa_r, out_sem, flood,
):
    s = lax.axis_index("sect")
    t = lax.axis_index("tp")
    k = t % 2
    x = (t // 2) % 4
    yh = t // 8
    g = t // 2
    z = s // 2
    yl = s % 2
    sib = (s, t + 1 - 2 * k)

    def ring_dst(i):
        dy, dx = RING[i]
        return ((yh + dy) % 2) * 4 + (x + dx) % 4

    def ring_src(i):
        dy, dx = RING[i]
        return ((yh + dy) % 2) * 4 + (x + 4 - dx) % 4

    def sect_peer(i):
        j = i // 2
        sign = 1 - 2 * (j % 2)
        dz = 8 + sign * ((j + 1) // 2)
        yx = 1 - i % 2
        return dz, yx

    def z_peer(dz, yx):
        return (((z + dz + 16) % 16) * 2 + (yl + yx) % 2, t)

    def remote(src, dst, ss, rr, dev):
        c = pltpu.make_async_remote_copy(
            src_ref=src, dst_ref=dst, send_sem=ss, recv_sem=rr, device_id=dev, device_id_type=MESH
        )
        c.start()
        return c

    def load(src, dst, sem):
        c = pltpu.make_async_copy(src, dst, sem)
        c.start()
        return c

    bar = pltpu.get_barrier_semaphore()
    greeted = [sib] + [(s, ring_dst(i) * 2 + k) for i in range(7)]
    greeted += [z_peer(1, 0), z_peer(-1, 0), z_peer(1, 1), z_peer(-1, 1), z_peer(0, 1)]
    for peer in greeted:
        pl.semaphore_signal(bar, inc=1, device_id=peer, device_id_type=MESH)

    order = [ring_dst(i) for i in range(7)] + [g]
    c_hid = load(hid, hraw, in_sem.at[0])
    c_gain = load(gain, graw, in_sem.at[1])
    c_w = [
        load(
            weight.at[:, pl.ds(pl.multiple_of(j * 2 * HD, 2 * HD), 2 * HD)], wv.at[j], w_sem.at[n]
        )
        for n, j in enumerate(order)
    ]
    c_pd = load(pdest, pdv, in_sem.at[2])
    c_doc = load(doc, docv, in_sem.at[3])
    c_tab = load(table, tabv, in_sem.at[4])
    c_ctx = load(ctx, ctxs, in_sem.at[5])
    c_old = load(oldp, oldbuf, in_sem.at[6])
    c_qp = load(qpre, qp, in_sem.at[7])
    c_qd = load(qdec, qd, in_sem.at[8])

    c_hid.wait()
    c_gain.wait()
    h = hraw[...].astype(F32).reshape(TOK // PAGE, PAGE, FEAT)
    h = jnp.concatenate([h[:, :HALF].reshape(CH, FEAT), h[:, HALF:].reshape(CH, FEAT)], axis=0)
    hs[...] = (h * graw[...].astype(F32).reshape(1, FEAT)).astype(BF16)
    hh = h * h
    folded = hh[:, 0:128] + hh[:, 128:256] + hh[:, 256:384] + hh[:, 384:512]
    sq_row = jnp.sum(folded.T, axis=0, keepdims=True)
    for q in range(4):
        st[k, q:q + 1, :] = sq_row[:, q * 128:(q + 1) * 128]
    st[k, 4:8, :] = jnp.zeros((4, 128), F32)

    blocks = [(c, n) for c in range(2) for n in range(8)]
    c_ps, c_rs, c_sq = {}, {}, {}
    c_st = None

    def signal_round(r):
        for sign in (1, -1):
            pl.semaphore_signal(
                flood.at[r], inc=1, device_id=z_peer(sign * (1 << r), 0), device_id_type=MESH
            )

    for q in range(16 + LAG):
        if q < 16:
            c, n = blocks[q]
            j = order[n]
            if c == 0:
                c_w[n].wait()
            both = dot(hs[c * CH:(c + 1) * CH, :], wv[j])
            part[c, j, 0] = both[:, :HD]
            part[c, j, 1] = both[:, HD:]
            if q == 0:
                pl.semaphore_wait(bar, len(greeted))
                c_st = remote(st.at[k], st.at[k], sib_s.at[0], sib_r.at[0], sib)
            c_ps[q] = remote(part.at[c, j, 1 - k], sibp.at[c, j], ps_s.at[q], ps_r.at[q], sib)
            if q == 0:
                signal_round(0)
        p = q - LAG
        if p < 0:
            continue
        if p == 0:
            c_st.wait_recv()
            chip_sq = st[0] + st[1]
            chip_col = lax.rsqrt(chip_sq * (1.0 / (2 * FEAT)) + TINY).T
        c, n = blocks[p]
        j = order[n]
        c_ps[p].wait_recv()
        total = part[c, j, k] + sibp[c, j]
        if n == 7:
            part[c, j, k] = total
            continue
        level = jnp.concatenate(
            [total[:128] * chip_col[:, 2 * c:2 * c + 1], total[128:] * chip_col[:, 2 * c + 1:2 * c + 2]],
            axis=0,
        )
        top = jnp.maximum(jnp.max(jnp.abs(level), axis=0, keepdims=True), TINY)
        sbuf[c, j] = jnp.round(level * (STEPS / top)).astype(jnp.int32).astype(jnp.int16)
        sstat[c, j] = chip_sq
        sstat[c, j, 4:5, :] = top * (1.0 / STEPS)
        peer = (s, j * 2 + k)
        c_sq[p] = remote(sstat.at[c, j], rstat.at[c, g], sq_s.at[c, n], sq_r.at[c, n], peer)
        c_rs[p] = remote(sbuf.at[c, j], rs.at[c, g], rs_s.at[c, n], rs_r.at[c, n], peer)

    pl.semaphore_wait(flood.at[0], 2)
    signal_round(1)

    c_pd.wait()
    eye = lax.broadcasted_iota(jnp.int32, (32, 32), 0) == lax.broadcasted_iota(jnp.int32, (32, 32), 1)
    page_col = jnp.sum(jnp.where(eye, jnp.broadcast_to(pdv[...], (32, 32)), 0), axis=1, keepdims=True)
    page_of = lax.broadcasted_iota(jnp.int32, (32, CH), 1) // HALF
    page_row = lax.broadcasted_iota(jnp.int32, (32, CH), 0)
    page_b = jnp.broadcast_to(page_col, (32, CH))
    dest_tok = jnp.sum(jnp.where(page_of == page_row, page_b, 0), axis=0, keepdims=True)
    rank_tok = jnp.sum(
        jnp.where((page_b == dest_tok) & (page_row < page_of), 1, 0), axis=0, keepdims=True
    )
    tok_in = lax.broadcasted_iota(jnp.int32, (1, CH), 1) % HALF
    target = (dest_tok * SLOTS + rank_tok) * HALF + tok_in
    for c in range(4):
        rows = lax.broadcasted_iota(jnp.int32, (128, CH), 0) + c * 128
        chooser[c * 128:(c + 1) * 128, :] = jnp.where(rows == target, 1.0, 0.0).astype(BF16)

    c_old.wait()
    for c in range(OLD // 32):
        blk = oldbuf[2 * c:2 * c + 2].reshape(32, 16, HD).astype(F32)
        head = lax.broadcasted_iota(jnp.int32, (1, 16, 1), 1)
        for m in range(2):
            one = jnp.sum(jnp.where(head == 2 * g + m, blk, 0.0), axis=1)
            oldkv[m, c * 32:(c + 1) * 32, :] = one.astype(BF16)

    pl.semaphore_wait(flood.at[1], 2)
    signal_round(2)

    c_tab.wait()
    c_ctx.wait()
    col = lax.broadcasted_iota(jnp.int32, (ROWS, OLD + FRESH), 1)
    fresh = col - OLD
    within = fresh % (FRESH // 2)
    col_slot = jnp.where(col < OLD, col // PAGE, 16 + within // HALF)
    col_in = jnp.where(col < OLD, col % PAGE, (fresh // (FRESH // 2)) * HALF + within % HALF)
    where_pos = jnp.full((ROWS, OLD + FRESH), 1 << 20, jnp.int32)
    tab = tabv[...]
    for j in range(MAXP):
        where_pos = jnp.where(tab[:, j:j + 1] == col_slot, j * PAGE + col_in, where_pos)
    row_id = lax.broadcasted_iota(jnp.int32, (ROWS, 1), 0)
    lens = jnp.zeros((ROWS, 1), jnp.int32)
    for r in range(ROWS):
        lens = jnp.where(row_id == r, ctxs[r], lens)
    pos[...] = jnp.where(where_pos < lens, 0.0, NEG)

    def page_copy(c, i):
        dz, yx = sect_peer(i)
        dst = ((z + dz) % 16) * 2 + (yl + yx) % 2
        return pltpu.make_async_remote_copy(
            src_ref=outg.at[c, pl.ds(pl.multiple_of(dst * MSG, MSG), MSG)],
            dst_ref=pool.at[k, c, pl.ds(pl.multiple_of(s * MSG, MSG), MSG)],
            send_sem=aa_s.at[c, i], recv_sem=aa_r.at[c, i], device_id=(dst, t), device_id_type=MESH,
        )

    def page_start(c):
        def body(i, _):
            page_copy(c, i).start()
            return 0
        lax.fori_loop(0, 31, body, 0)

    def page_wait(c):
        def body(i, _):
            page_copy(c, i).wait_recv()
            return 0
        lax.fori_loop(0, 31, body, 0)

    def page_sent(c):
        def body(i, _):
            page_copy(c, i).wait_send()
            return 0
        lax.fori_loop(0, 31, body, 0)

    own = pl.ds(pl.multiple_of(s * MSG, MSG), MSG)
    for c in range(2):
        upper = part[c, g, k, 0:128]
        lower = part[c, g, k, 128:256]
        total_sq = chip_sq
        for i in (5, 6, 3, 4, 1, 2, 0):
            p = c * 8 + i
            c_sq[p].wait_recv()
            src = ring_src(i)
            stat = rstat[c, src]
            total_sq = total_sq + stat
            ms = stat * (1.0 / (2 * FEAT)) + TINY
            scale = (ms * lax.rsqrt(ms)).T
            col_scale = stat[4:5, :]
            c_rs[p].wait_recv()
            got = rs[c, src].astype(jnp.int32).astype(F32) * col_scale
            upper = upper + got[:128] * scale[:, 2 * c:2 * c + 1]
            lower = lower + got[128:] * scale[:, 2 * c + 1:2 * c + 2]
        inv = lax.rsqrt(total_sq / D + NORM_EPS).T
        kvc[c, 0:128] = (upper * inv[:, 2 * c:2 * c + 1]).astype(BF16)
        kvc[c, 128:256] = (lower * inv[:, 2 * c + 1:2 * c + 2]).astype(BF16)
        if c == 0:
            pl.semaphore_wait(flood.at[2], 2)
        for r in range(2):
            outg[c, r * 256:(r + 1) * 256] = dot(chooser[r * 256:(r + 1) * 256, :], kvc[c]).astype(BF16)
        page_start(c)
        pool[k, c, own, :] = outg[c, own, :]
    halves = [kvc[c].astype(F32).reshape(TOK // PAGE, HALF, HD) for c in range(2)]
    kvh[k] = jnp.concatenate(halves, axis=1).reshape(TOK, HD).astype(BF16)
    c_kv = remote(kvh.at[k], kvh.at[k], sib_s.at[1], sib_r.at[1], sib)

    c_qp.wait()
    c_doc.wait()
    doc_row = docv[...].astype(F32)
    doc_col = jnp.broadcast_to(doc_row, (8, TOK)).T[:, 0:1]
    c_kv.wait_recv()
    out_copies = []
    for b in range(4):
        lo, hi = max(0, b - 2) * 128, (b + 1) * 128
        q0 = b * 128
        tq = lax.broadcasted_iota(jnp.int32, (128, hi - lo), 0) + q0
        tk = lax.broadcasted_iota(jnp.int32, (128, hi - lo), 1) + lo
        allowed = (doc_col[q0:hi, :] == doc_row[:, lo:hi]) & (tk <= tq)
        keys = kvh[0, lo:hi, :]
        values = kvh[1, lo:hi, :]
        for n in range(NH):
            sc = dot_t(qp[q0:hi, n * HD:(n + 1) * HD], keys) * SCALE
            wts = softmax_weights(jnp.where(allowed, sc, NEG))
            obuf[q0:hi, n * HD:(n + 1) * HD] = dot(wts, values).astype(BF16)
        out_copies.append(load(obuf.at[q0:hi], o_pre.at[q0:hi], out_sem.at[b]))

    c_qd.wait()
    qs = jnp.concatenate([qd[:, n * HD:(n + 1) * HD] for n in range(NH)], axis=0)
    mask = jnp.concatenate([pos[...]] * NH, axis=0)
    score = [dot_t(qs, oldkv[0]) * SCALE + mask[:, :OLD]]
    peak = jnp.max(score[0], axis=-1, keepdims=True)
    half = FRESH // 2
    c_pool = []
    for c in range(2):
        page_wait(c)
        c_pool.append(remote(pool.at[k, c], pool.at[k, c], sib_s.at[2 + c], sib_r.at[2 + c], sib))
    for c in range(2):
        c_pool[c].wait_recv()
        sc = dot_t(qs, pool[0, c]) * SCALE + mask[:, OLD + c * half:OLD + (c + 1) * half]
        score.append(sc)
        peak = jnp.maximum(peak, jnp.max(sc, axis=-1, keepdims=True))
    raised = [jnp.exp(sc - peak) for sc in score]
    norm = sum(jnp.sum(e, axis=-1, keepdims=True) for e in raised)
    norm = 1.0 / norm
    mixed = dot((raised[0] * norm).astype(BF16), oldkv[1])
    for c in range(2):
        mixed = mixed + dot((raised[1 + c] * norm).astype(BF16), pool[1, c])
    mixed = mixed.astype(BF16)
    for n in range(NH):
        dbuf[:, n * HD:(n + 1) * HD] = mixed[n * ROWS:(n + 1) * ROWS]
    out_copies.append(load(dbuf, o_dec, out_sem.at[4]))

    for c in [c_st, c_kv] + c_pool + list(c_ps.values()) + list(c_rs.values()) + list(c_sq.values()):
        c.wait_send()
    page_sent(0)
    page_sent(1)
    for c in out_copies:
        c.wait()


def local(hidden_pre, norm_gain, kv_weight, query_pre, doc_ids, page_dest, old_pages, query_dec, page_table, ctx_len):
    any_spec = pl.BlockSpec(memory_space=pl.ANY)
    dma = pltpu.SemaphoreType.DMA
    vm = pltpu.VMEM
    I32 = jnp.int32
    I16 = jnp.int16
    return pl.pallas_call(
        kernel,
        name="serve",
        out_shape=(
            jax.ShapeDtypeStruct((TOK, NH * HD), BF16),
            jax.ShapeDtypeStruct((ROWS, NH * HD), BF16),
        ),
        in_specs=[any_spec] * 10,
        out_specs=(any_spec, any_spec),
        scratch_shapes=[
            vm((TOK, FEAT), BF16), vm((FEAT,), BF16), vm((CHIPS, FEAT, 2 * HD), BF16),
            vm((1, TOK), I32), vm((1, 32), I32), vm((ROWS, MAXP), I32), pltpu.SMEM((ROWS,), I32),
            vm((TOK, FEAT), BF16), vm((2, 8, 128), F32),
            vm((2, CHIPS, 2, CH, HD), F32), vm((2, CHIPS, CH, HD), F32),
            vm((2, CHIPS, CH, HD), I16), vm((2, CHIPS, CH, HD), I16),
            vm((2, CHIPS, 8, HD), F32), vm((2, CHIPS, 8, HD), F32),
            vm((FRESH // 2, CH), BF16), vm((2, CH, HD), BF16), vm((2, FRESH // 2, HD), BF16),
            vm((2, TOK, HD), BF16), vm((2, 2, FRESH // 2, HD), BF16),
            vm((16, 16, 16, HD), BF16), vm((2, OLD, HD), BF16), vm((TOK, NH * HD), BF16),
            vm((ROWS, NH * HD), BF16), vm((ROWS, OLD + FRESH), F32),
            vm((TOK, NH * HD), BF16), vm((ROWS, NH * HD), BF16),
            dma((9,)), dma((8,)), dma((4,)), dma((4,)), dma((16,)), dma((16,)), dma((2, 7)), dma((2, 7)),
            dma((2, 7)), dma((2, 7)), dma((2, 31)), dma((2, 31)), dma((5,)), pltpu.SemaphoreType.REGULAR((3,)),
        ],
        compiler_params=pltpu.CompilerParams(
            collective_id=0, has_side_effects=True, vmem_limit_bytes=VMEM_LIMIT
        ),
    )(
        hidden_pre, norm_gain, kv_weight, query_pre, doc_ids, page_dest.reshape(1, 32), old_pages,
        query_dec, page_table, ctx_len,
    )


def solution(mesh):
    in_specs = (
        P("sect", "tp"),
        P("tp"),
        P("tp", None),
        P("sect", "tp"),
        P("sect", None),
        P("sect", None),
        P("sect", None, None, None),
        P("sect", "tp"),
        P("sect", None),
        P("sect"),
    )
    out_specs = (P("sect", "tp"), P("sect", "tp"))
    return jax.shard_map(local, mesh=mesh, in_specs=in_specs, out_specs=out_specs, check_vma=False)
```

time: 60.5 us -> 51.7 us (0.85)
  Pallas kernels: 56.4 us -> 47.7 us
    pallas_call x1, Pallas kernels: 56.4 us -> 47.7 us  [local(): pl.pallas_call(kernel, name='serve', out_shape=(jax.ShapeDtypeStruct((TOK...]
where the time goes in v2:
time: 51.7 us; the launch traced here: 51.5 us
  Pallas kernels  47.7 us (92%)
  local copies, waits for them, and re-layouts  3.19 us (6%)
  between operations  0.64 us (1%)
    pallas_call x1, Pallas kernels, local(): pl.pallas_call(kernel, name='serve', out_shape=(jax.ShapeDtypeStruct((TOK...  47.7 us
    unnamed x2, local copies, waits for them, and re-layouts  3.19 us

profile of v2, /device:TPU:1, one launch (start us, length us, event | category | flops | bytes accessed | tf_op | source)
XLA Modules:
  0.0 51.5 jit_solution(7572204059087004407)
XLA Ops:
  0.6 47.7 %serve.1 = (bf16[512,512]{1,0:T(8,128)(2,1)}, bf16[16,512]{1,0:T(8,128)(2,1)}) custom-call(bf16[512,512]{1,0:T(8,128)(2,1)} %hid.1, bf16[512]{0:T(512)(128)(2,1)} %gain.1, bf16[512,2048]{1,0:T(8,128)(2,1)} %weight.1, bf16[512,512]{1,0:T(8,128)(2,1)} %qpre.1, s32[1,512]{1,0:T(1,128)} %doc.1, s32[1,32]{1,0:T(1,128)} %bitcast.1, ...), custom_call_target="tpu_custom_call" | custom-call | tf_op jit(solution)/shard_map/serve/pallas_call | solution.py:349
  48.3 1.9 %copy.14 = bf16[512,512]{1,0:T(8,128)(2,1)} copy(bf16[512,512]{1,0:T(8,128)(2,1)} %get-tuple-element.4) | data formatting | bytes 1048576
  50.2 1.3 %copy.15 = bf16[16,512]{1,0:T(8,128)(2,1)} copy(bf16[16,512]{1,0:T(8,128)(2,1)} %get-tuple-element.5) | data formatting | bytes 32768

commit v3 on v2

--- a/solution.py
+++ b/solution.py
@@ -18,6 +18,7 @@
 MSG = SLOTS * HALF
 FRESH = SECT * SLOTS * PAGE
 LAG = 3
+AHEAD = 6
 ROWS = 16
 NH = 4
 OLD = 256
@@ -73,13 +74,6 @@
         dy, dx = RING[i]
         return ((yh + dy) % 2) * 4 + (x + 4 - dx) % 4
 
-    def sect_peer(i):
-        j = i // 2
-        sign = 1 - 2 * (j % 2)
-        dz = 8 + sign * ((j + 1) // 2)
-        yx = 1 - i % 2
-        return dz, yx
-
     def z_peer(dz, yx):
         return (((z + dz + 16) % 16) * 2 + (yl + yx) % 2, t)
 
@@ -140,6 +134,12 @@
                 flood.at[r], inc=1, device_id=z_peer(sign * (1 << r), 0), device_id_type=MESH
             )
 
+    def swap(q):
+        c, n = blocks[q]
+        j = order[n]
+        c_ps[q] = remote(part.at[c, j, 1 - k], sibp.at[c, j], ps_s.at[q], ps_r.at[q], sib)
+
+    done = 0
     for q in range(16 + LAG):
         if q < 16:
             c, n = blocks[q]
@@ -149,40 +149,47 @@
             both = dot(hs[c * CH:(c + 1) * CH, :], wv[j])
             part[c, j, 0] = both[:, :HD]
             part[c, j, 1] = both[:, HD:]
-            if q == 0:
-                pl.semaphore_wait(bar, len(greeted))
-                c_st = remote(st.at[k], st.at[k], sib_s.at[0], sib_r.at[0], sib)
-            c_ps[q] = remote(part.at[c, j, 1 - k], sibp.at[c, j], ps_s.at[q], ps_r.at[q], sib)
-            if q == 0:
-                signal_round(0)
-        p = q - LAG
-        if p < 0:
+        if q < AHEAD - 1:
             continue
-        if p == 0:
-            c_st.wait_recv()
-            chip_sq = st[0] + st[1]
-            chip_col = lax.rsqrt(chip_sq * (1.0 / (2 * FEAT)) + TINY).T
-        c, n = blocks[p]
-        j = order[n]
-        c_ps[p].wait_recv()
-        total = part[c, j, k] + sibp[c, j]
-        if n == 7:
-            part[c, j, k] = total
-            continue
-        level = jnp.concatenate(
-            [total[:128] * chip_col[:, 2 * c:2 * c + 1], total[128:] * chip_col[:, 2 * c + 1:2 * c + 2]],
-            axis=0,
-        )
-        top = jnp.maximum(jnp.max(jnp.abs(level), axis=0, keepdims=True), TINY)
-        sbuf[c, j] = jnp.round(level * (STEPS / top)).astype(jnp.int32).astype(jnp.int16)
-        sstat[c, j] = chip_sq
-        sstat[c, j, 4:5, :] = top * (1.0 / STEPS)
-        peer = (s, j * 2 + k)
-        c_sq[p] = remote(sstat.at[c, j], rstat.at[c, g], sq_s.at[c, n], sq_r.at[c, n], peer)
-        c_rs[p] = remote(sbuf.at[c, j], rs.at[c, g], rs_s.at[c, n], rs_r.at[c, n], peer)
-
-    pl.semaphore_wait(flood.at[0], 2)
-    signal_round(1)
+        if q == AHEAD - 1:
+            pl.semaphore_wait(bar, len(greeted))
+            c_st = remote(st.at[k], st.at[k], sib_s.at[0], sib_r.at[0], sib)
+            signal_round(0)
+            for early in range(AHEAD):
+                swap(early)
+        elif q < 16:
+            swap(q)
+        while done <= q - LAG:
+            p = done
+            done += 1
+            if p == 0:
+                c_st.wait_recv()
+                chip_sq = st[0] + st[1]
+                chip_col = lax.rsqrt(chip_sq * (1.0 / (2 * FEAT)) + TINY).T
+            c, n = blocks[p]
+            j = order[n]
+            c_ps[p].wait_recv()
+            total = part[c, j, k] + sibp[c, j]
+            if n == 7:
+                part[c, j, k] = total
+                continue
+            level = jnp.concatenate(
+                [
+                    total[:128] * chip_col[:, 2 * c:2 * c + 1],
+                    total[128:] * chip_col[:, 2 * c + 1:2 * c + 2],
+                ],
+                axis=0,
+            )
+            top = jnp.maximum(jnp.max(jnp.abs(level), axis=0, keepdims=True), TINY)
+            sbuf[c, j] = jnp.round(level * (STEPS / top)).astype(jnp.int32).astype(jnp.int16)
+            sstat[c, j] = chip_sq
+            sstat[c, j, 4:5, :] = top * (1.0 / STEPS)
+            peer = (s, j * 2 + k)
+            c_sq[p] = remote(sstat.at[c, j], rstat.at[c, g], sq_s.at[c, n], sq_r.at[c, n], peer)
+            c_rs[p] = remote(sbuf.at[c, j], rs.at[c, g], rs_s.at[c, n], rs_r.at[c, n], peer)
+        if q == 10:
+            pl.semaphore_wait(flood.at[0], 2)
+            signal_round(1)
 
     c_pd.wait()
     eye = lax.broadcasted_iota(jnp.int32, (32, 32), 0) == lax.broadcasted_iota(jnp.int32, (32, 32), 1)
@@ -229,12 +236,11 @@
     pos[...] = jnp.where(where_pos < lens, 0.0, NEG)
 
     def page_copy(c, i):
-        dz, yx = sect_peer(i)
-        dst = ((z + dz) % 16) * 2 + (yl + yx) % 2
+        dst = i + (SECT + i - s) // SECT
         return pltpu.make_async_remote_copy(
             src_ref=outg.at[c, pl.ds(pl.multiple_of(dst * MSG, MSG), MSG)],
             dst_ref=pool.at[k, c, pl.ds(pl.multiple_of(s * MSG, MSG), MSG)],
-            send_sem=aa_s.at[c, i], recv_sem=aa_r.at[c, i], device_id=(dst, t), device_id_type=MESH,
+            send_sem=aa_s.at[c], recv_sem=aa_r.at[c], device_id=(dst, t), device_id_type=MESH,
         )
 
     def page_start(c):
@@ -243,37 +249,35 @@
             return 0
         lax.fori_loop(0, 31, body, 0)
 
-    def page_wait(c):
-        def body(i, _):
-            page_copy(c, i).wait_recv()
-            return 0
-        lax.fori_loop(0, 31, body, 0)
-
-    def page_sent(c):
-        def body(i, _):
-            page_copy(c, i).wait_send()
-            return 0
-        lax.fori_loop(0, 31, body, 0)
+    def pages_all(c):
+        most = pl.ds(0, 31 * MSG)
+        return pltpu.make_async_remote_copy(
+            src_ref=outg.at[c, most], dst_ref=pool.at[k, c, most],
+            send_sem=aa_s.at[c], recv_sem=aa_r.at[c], device_id=sib, device_id_type=MESH,
+        )
 
     own = pl.ds(pl.multiple_of(s * MSG, MSG), MSG)
+    total_sq = chip_sq
+    scales = {}
     for c in range(2):
         upper = part[c, g, k, 0:128]
         lower = part[c, g, k, 128:256]
-        total_sq = chip_sq
         for i in (5, 6, 3, 4, 1, 2, 0):
             p = c * 8 + i
             c_sq[p].wait_recv()
             src = ring_src(i)
             stat = rstat[c, src]
-            total_sq = total_sq + stat
-            ms = stat * (1.0 / (2 * FEAT)) + TINY
-            scale = (ms * lax.rsqrt(ms)).T
+            if c == 0:
+                total_sq = total_sq + stat
+                ms = stat * (1.0 / (2 * FEAT)) + TINY
+                scales[i] = (ms * lax.rsqrt(ms)).T
             col_scale = stat[4:5, :]
             c_rs[p].wait_recv()
             got = rs[c, src].astype(jnp.int32).astype(F32) * col_scale
-            upper = upper + got[:128] * scale[:, 2 * c:2 * c + 1]
-            lower = lower + got[128:] * scale[:, 2 * c + 1:2 * c + 2]
-        inv = lax.rsqrt(total_sq / D + NORM_EPS).T
+            upper = upper + got[:128] * scales[i][:, 2 * c:2 * c + 1]
+            lower = lower + got[128:] * scales[i][:, 2 * c + 1:2 * c + 2]
+        if c == 0:
+            inv = lax.rsqrt(total_sq / D + NORM_EPS).T
         kvc[c, 0:128] = (upper * inv[:, 2 * c:2 * c + 1]).astype(BF16)
         kvc[c, 128:256] = (lower * inv[:, 2 * c + 1:2 * c + 2]).astype(BF16)
         if c == 0:
@@ -313,8 +317,10 @@
     peak = jnp.max(score[0], axis=-1, keepdims=True)
     half = FRESH // 2
     c_pool = []
+    for c in [c_st] + list(c_ps.values()) + list(c_rs.values()) + list(c_sq.values()):
+        c.wait_send()
     for c in range(2):
-        page_wait(c)
+        pages_all(c).wait_recv()
         c_pool.append(remote(pool.at[k, c], pool.at[k, c], sib_s.at[2 + c], sib_r.at[2 + c], sib))
     for c in range(2):
         c_pool[c].wait_recv()
@@ -332,10 +338,10 @@
         dbuf[:, n * HD:(n + 1) * HD] = mixed[n * ROWS:(n + 1) * ROWS]
     out_copies.append(load(dbuf, o_dec, out_sem.at[4]))
 
-    for c in [c_st, c_kv] + c_pool + list(c_ps.values()) + list(c_rs.values()) + list(c_sq.values()):
+    for c in [c_kv] + c_pool:
         c.wait_send()
-    page_sent(0)
-    page_sent(1)
+    for c in range(2):
+        pages_all(c).wait_send()
     for c in out_copies:
         c.wait()
 
@@ -368,7 +374,7 @@
             vm((ROWS, NH * HD), BF16), vm((ROWS, OLD + FRESH), F32),
             vm((TOK, NH * HD), BF16), vm((ROWS, NH * HD), BF16),
             dma((9,)), dma((8,)), dma((4,)), dma((4,)), dma((16,)), dma((16,)), dma((2, 7)), dma((2, 7)),
-            dma((2, 7)), dma((2, 7)), dma((2, 31)), dma((2, 31)), dma((5,)), pltpu.SemaphoreType.REGULAR((3,)),
+            dma((2, 7)), dma((2, 7)), dma((2,)), dma((2,)), dma((5,)), pltpu.SemaphoreType.REGULAR((3,)),
         ],
         compiler_params=pltpu.CompilerParams(
             collective_id=0, has_side_effects=True, vmem_limit_bytes=VMEM_LIMIT

time: 51.7 us -> 47.8 us (0.925)
  Pallas kernels: 47.7 us -> 43.8 us
    pallas_call x1, Pallas kernels: 47.7 us -> 43.8 us  [local(): pl.pallas_call(kernel, name='serve', out_shape=(jax.ShapeDtypeStruct((TOK...]
where the time goes in v3:
time: 47.8 us; the launch traced here: 47.6 us
  Pallas kernels  43.8 us (92%)
  local copies, waits for them, and re-layouts  3.19 us (7%)
  between operations  0.64 us (1%)
    pallas_call x1, Pallas kernels, local(): pl.pallas_call(kernel, name='serve', out_shape=(jax.ShapeDtypeStruct((TOK...  43.8 us
    unnamed x2, local copies, waits for them, and re-layouts  3.19 us

profile of v3, /device:TPU:1, one launch (start us, length us, event | category | flops | bytes accessed | tf_op | source)
XLA Modules:
  0.0 47.6 jit_solution(1857889618833965055)
XLA Ops:
  0.6 43.8 %serve.1 = (bf16[512,512]{1,0:T(8,128)(2,1)}, bf16[16,512]{1,0:T(8,128)(2,1)}) custom-call(bf16[512,512]{1,0:T(8,128)(2,1)} %hid.1, bf16[512]{0:T(512)(128)(2,1)} %gain.1, bf16[512,2048]{1,0:T(8,128)(2,1)} %weight.1, bf16[512,512]{1,0:T(8,128)(2,1)} %qpre.1, s32[1,512]{1,0:T(1,128)} %doc.1, s32[1,32]{1,0:T(1,128)} %bitcast.1, ...), custom_call_target="tpu_custom_call" | custom-call | tf_op jit(solution)/shard_map/serve/pallas_call | solution.py:355
  44.4 1.9 %copy.14 = bf16[512,512]{1,0:T(8,128)(2,1)} copy(bf16[512,512]{1,0:T(8,128)(2,1)} %get-tuple-element.4) | data formatting | bytes 1048576
  46.3 1.3 %copy.15 = bf16[16,512]{1,0:T(8,128)(2,1)} copy(bf16[16,512]{1,0:T(8,128)(2,1)} %get-tuple-element.5) | data formatting | bytes 32768

commit v4 on v3

--- a/solution.py
+++ b/solution.py
@@ -17,8 +17,11 @@
 CH = TOK // 2
 MSG = SLOTS * HALF
 FRESH = SECT * SLOTS * PAGE
-LAG = 3
-AHEAD = 6
+LAG = 2
+AHEAD = 3
+EARLY = 6
+RH = CH // 2
+KEYS = ((1, 2), (0, 2), (1, 1), (0, 1), (1, 0), (1, 3), (0, 3), (0, 0))
 ROWS = 16
 NH = 4
 OLD = 256
@@ -28,7 +31,6 @@
 MESH = pl.DeviceIdType.MESH
 F32 = jnp.float32
 BF16 = jnp.bfloat16
-RING = ((1, 2), (1, 1), (1, 3), (0, 2), (1, 0), (0, 1), (0, 3))
 NEG = -jnp.inf
 TINY = 1e-30
 STEPS = 32000.0
@@ -52,8 +54,8 @@
 def kernel(
     hid, gain, weight, qpre, doc, pdest, oldp, qdec, table, ctx,
     o_pre, o_dec,
-    hraw, graw, wv, docv, pdv, tabv, ctxs, hs, st, part, sibp, sbuf, rs, sstat, rstat, chooser, kvc, outg, kvh, pool,
-    oldbuf, oldkv, qp, qd, pos, obuf, dbuf,
+    hraw, graw, wv, docv, pdv, tabv, ctxs, hs, st, part, sibp, sbuf, sbuf2, rs, nsend, nrecv, rowb, chooser, kvc, outg, kvh, pool,
+    oldbuf, oldkv, qp, qd, pos, obuf,
     in_sem, w_sem, sib_s, sib_r, ps_s, ps_r, rs_s, rs_r, sq_s, sq_r, aa_s, aa_r, out_sem, flood,
 ):
     s = lax.axis_index("sect")
@@ -66,13 +68,11 @@
     yl = s % 2
     sib = (s, t + 1 - 2 * k)
 
-    def ring_dst(i):
-        dy, dx = RING[i]
-        return ((yh + dy) % 2) * 4 + (x + dx) % 4
-
-    def ring_src(i):
-        dy, dx = RING[i]
-        return ((yh + dy) % 2) * 4 + (x + 4 - dx) % 4
+    def head(rel, dx):
+        return ((yh + rel) % 2) * 4 + (x + dx) % 4
+
+    def chip(rel, dx):
+        return (s, head(rel, dx) * 2 + k)
 
     def z_peer(dz, yx):
         return (((z + dz + 16) % 16) * 2 + (yl + yx) % 2, t)
@@ -90,20 +90,19 @@
         return c
 
     bar = pltpu.get_barrier_semaphore()
-    greeted = [sib] + [(s, ring_dst(i) * 2 + k) for i in range(7)]
+    greeted = [sib, chip(1, 0), chip(0, 1), chip(0, 2), chip(0, 3)]
     greeted += [z_peer(1, 0), z_peer(-1, 0), z_peer(1, 1), z_peer(-1, 1), z_peer(0, 1)]
     for peer in greeted:
         pl.semaphore_signal(bar, inc=1, device_id=peer, device_id_type=MESH)
 
-    order = [ring_dst(i) for i in range(7)] + [g]
     c_hid = load(hid, hraw, in_sem.at[0])
     c_gain = load(gain, graw, in_sem.at[1])
-    c_w = [
-        load(
+    c_w = {}
+    for n, key in enumerate(KEYS):
+        j = head(*key)
+        c_w[key] = load(
             weight.at[:, pl.ds(pl.multiple_of(j * 2 * HD, 2 * HD), 2 * HD)], wv.at[j], w_sem.at[n]
         )
-        for n, j in enumerate(order)
-    ]
     c_pd = load(pdest, pdv, in_sem.at[2])
     c_doc = load(doc, docv, in_sem.at[3])
     c_tab = load(table, tabv, in_sem.at[4])
@@ -124,9 +123,8 @@
         st[k, q:q + 1, :] = sq_row[:, q * 128:(q + 1) * 128]
     st[k, 4:8, :] = jnp.zeros((4, 128), F32)
 
-    blocks = [(c, n) for c in range(2) for n in range(8)]
-    c_ps, c_rs, c_sq = {}, {}, {}
-    c_st = None
+    c_ps, sends, inbox, notes = {}, [], {}, {}
+    nsend[...] = jnp.zeros(nsend.shape, F32)
 
     def signal_round(r):
         for sign in (1, -1):
@@ -134,62 +132,157 @@
                 flood.at[r], inc=1, device_id=z_peer(sign * (1 << r), 0), device_id_type=MESH
             )
 
-    def swap(q):
-        c, n = blocks[q]
-        j = order[n]
-        c_ps[q] = remote(part.at[c, j, 1 - k], sibp.at[c, j], ps_s.at[q], ps_r.at[q], sib)
-
+    def norm_col(sq):
+        return lax.rsqrt(sq * (1.0 / (2 * FEAT)) + TINY).T
+
+    def scale_col(sq):
+        ms = sq * (1.0 / (2 * FEAT)) + TINY
+        return (ms * lax.rsqrt(ms)).T
+
+    def spread(cols, quarter):
+        return jnp.broadcast_to(cols[:, quarter:quarter + 1], (RH, HD))
+
+    def code(level):
+        top = jnp.maximum(jnp.max(jnp.abs(level), axis=0, keepdims=True), TINY)
+        return jnp.round(level * (STEPS / top)).astype(jnp.int32).astype(jnp.int16), top * (1.0 / STEPS)
+
+    def post(key, src, dst, index, peer):
+        inbox[key] = remote(src, dst, rs_s.at[index], rs_r.at[index], peer)
+        sends.append(inbox[key])
+
+    def post_first(c, rel, dx):
+        j = head(rel, dx)
+        if rel == 1:
+            post((c, "up", dx), sbuf.at[j, pl.ds(c * CH, RH)], rs.at[c, dx], c * 14 + dx, chip(1, 0))
+        if dx > 0:
+            slot = 4 + 2 * (dx - 1) + rel
+            post(
+                (c, "low", rel, dx), sbuf.at[j, pl.ds(c * CH + RH, RH)], rs.at[c, slot], c * 14 + slot,
+                chip(0, dx),
+            )
+
+    def post_note(note, sq, lines, peer):
+        nsend[note, 0:4, :] = sq[0:4]
+        for line, value in lines:
+            nsend[note, line:line + 1, :] = value
+        notes[note] = remote(nsend.at[note], nrecv.at[note], sq_s.at[note], sq_r.at[note], peer)
+        sends.append(notes[note])
+
+    def decode(c, slot, stat, line):
+        return rs[c, slot].astype(jnp.int32).astype(F32) * stat[line:line + 1, :]
+
+    steps = {}
     done = 0
-    for q in range(16 + LAG):
-        if q < 16:
-            c, n = blocks[q]
-            j = order[n]
-            if c == 0:
-                c_w[n].wait()
-            both = dot(hs[c * CH:(c + 1) * CH, :], wv[j])
-            part[c, j, 0] = both[:, :HD]
-            part[c, j, 1] = both[:, HD:]
+    for q in range(8 + LAG):
+        if q < 8:
+            j = head(*KEYS[q])
+            c_w[KEYS[q]].wait()
+            both = dot(hs[...], wv[j])
+            part[j, 0] = both[:, :HD]
+            part[j, 1] = both[:, HD:]
         if q < AHEAD - 1:
             continue
         if q == AHEAD - 1:
             pl.semaphore_wait(bar, len(greeted))
             c_st = remote(st.at[k], st.at[k], sib_s.at[0], sib_r.at[0], sib)
             signal_round(0)
-            for early in range(AHEAD):
-                swap(early)
-        elif q < 16:
-            swap(q)
+        for p in range(q if q >= AHEAD else 0, q + 1):
+            if p < 8:
+                j = head(*KEYS[p])
+                c_ps[p] = remote(part.at[j, 1 - k], sibp.at[j], ps_s.at[p], ps_r.at[p], sib)
         while done <= q - LAG:
             p = done
             done += 1
             if p == 0:
                 c_st.wait_recv()
                 chip_sq = st[0] + st[1]
-                chip_col = lax.rsqrt(chip_sq * (1.0 / (2 * FEAT)) + TINY).T
-            c, n = blocks[p]
-            j = order[n]
+                chip_col = norm_col(chip_sq)
+                for quarter in range(4):
+                    rowb[quarter * RH:(quarter + 1) * RH] = spread(chip_col, quarter)
+            rel, dx = KEYS[p]
+            j = head(rel, dx)
             c_ps[p].wait_recv()
-            total = part[c, j, k] + sibp[c, j]
-            if n == 7:
-                part[c, j, k] = total
+            total = part[j, k] + sibp[j]
+            part[j, k] = total
+            if (rel, dx) == (0, 0):
                 continue
-            level = jnp.concatenate(
-                [
-                    total[:128] * chip_col[:, 2 * c:2 * c + 1],
-                    total[128:] * chip_col[:, 2 * c + 1:2 * c + 2],
-                ],
-                axis=0,
-            )
-            top = jnp.maximum(jnp.max(jnp.abs(level), axis=0, keepdims=True), TINY)
-            sbuf[c, j] = jnp.round(level * (STEPS / top)).astype(jnp.int32).astype(jnp.int16)
-            sstat[c, j] = chip_sq
-            sstat[c, j, 4:5, :] = top * (1.0 / STEPS)
-            peer = (s, j * 2 + k)
-            c_sq[p] = remote(sstat.at[c, j], rstat.at[c, g], sq_s.at[c, n], sq_r.at[c, n], peer)
-            c_rs[p] = remote(sbuf.at[c, j], rs.at[c, g], rs_s.at[c, n], rs_r.at[c, n], peer)
-        if q == 10:
-            pl.semaphore_wait(flood.at[0], 2)
-            signal_round(1)
+            if p == 2:
+                pl.semaphore_wait(flood.at[0], 2)
+                signal_round(1)
+            sbuf[j], steps[rel, dx] = code(total * rowb[...])
+            post_first(0, rel, dx)
+            if (rel, dx) == (1, 3):
+                post_note(0, chip_sq, [(4 + n, steps[1, n]) for n in range(4)], chip(1, 0))
+            if rel == 0:
+                post_note(dx, chip_sq, [(4, steps[0, dx]), (5, steps[1, dx])], chip(0, dx))
+    for rel, dx in KEYS:
+        post_first(1, rel, dx)
+    pl.semaphore_wait(flood.at[1], 2)
+    signal_round(2)
+
+    known = {}
+
+    def second_step(c):
+        if c == 0:
+            notes[0].wait_recv()
+            stat = nrecv[0]
+            known["row_sq"] = chip_sq + stat
+            known["row_col"] = norm_col(known["row_sq"])
+            known["up"] = scale_col(stat)
+        for dx in (2, 1, 3):
+            inbox[c, "up", dx].wait_recv()
+        scale = spread(known["up"], 2 * c)
+        norm = spread(known["row_col"], 2 * c)
+        lines = {}
+        for dx in (2, 1, 3):
+            value = decode(c, dx, nrecv[0], 4 + dx) * scale + part[head(0, dx), k, c * CH:c * CH + RH]
+            sbuf2[c, dx - 1], lines[dx] = code(value * norm)
+        for dx in (2, 1, 3):
+            post((c, dx), sbuf2.at[c, dx - 1], rs.at[c, 9 + dx], c * 14 + 9 + dx, chip(0, dx))
+            post_note(3 + 4 * c + dx, known["row_sq"], [(4, lines[dx])], chip(0, dx))
+        if c == 0:
+            quad_sq = chip_sq
+            for dx in (2, 1, 3):
+                notes[dx].wait_recv()
+                stat = nrecv[dx]
+                known[dx] = scale_col(stat)
+                quad_sq = quad_sq + stat
+            known["quad_sq"] = quad_sq
+            known["quad_col"] = norm_col(quad_sq)
+        for dx in (2, 1, 3):
+            inbox[c, "low", 1, dx].wait_recv()
+        value = part[head(1, 0), k, c * CH + RH:(c + 1) * CH]
+        for dx in (2, 1, 3):
+            value = value + decode(c, 5 + 2 * (dx - 1), nrecv[dx], 5) * spread(known[dx], 2 * c + 1)
+        sbuf2[c, 3], line = code(value * spread(known["quad_col"], 2 * c + 1))
+        post((c, 13), sbuf2.at[c, 3], rs.at[c, 13], c * 14 + 13, chip(1, 0))
+        post_note(7 + 4 * c, known["quad_sq"], [(4, line)], chip(1, 0))
+
+    def last_step(c):
+        for dx in (1, 3, 2):
+            notes[3 + 4 * c + dx].wait_recv()
+        if c == 0:
+            total_sq = known["row_sq"]
+            for dx in (1, 3, 2):
+                known[3 + dx] = scale_col(nrecv[3 + dx])
+                total_sq = total_sq + nrecv[3 + dx]
+            known["inv"] = lax.rsqrt(total_sq / D + NORM_EPS).T
+        inbox[c, "up", 0].wait_recv()
+        for dx in (1, 2, 3):
+            inbox[c, "low", 0, dx].wait_recv()
+            inbox[c, dx].wait_recv()
+        notes[7 + 4 * c].wait_recv()
+        inbox[c, 13].wait_recv()
+        if c == 0:
+            known[7] = scale_col(nrecv[7])
+        top = decode(c, 0, nrecv[0], 4) * spread(known["up"], 2 * c) + part[g, k, c * CH:c * CH + RH]
+        low = part[g, k, c * CH + RH:(c + 1) * CH]
+        for dx in (1, 3, 2):
+            top = top + decode(c, 9 + dx, nrecv[3 + 4 * c + dx], 4) * spread(known[3 + dx], 2 * c)
+            low = low + decode(c, 4 + 2 * (dx - 1), nrecv[dx], 4) * spread(known[dx], 2 * c + 1)
+        low = low + decode(c, 13, nrecv[7 + 4 * c], 4) * spread(known[7], 2 * c + 1)
+        kvc[c, 0:RH] = (top * spread(known["inv"], 2 * c)).astype(BF16)
+        kvc[c, RH:CH] = (low * spread(known["inv"], 2 * c + 1)).astype(BF16)
 
     c_pd.wait()
     eye = lax.broadcasted_iota(jnp.int32, (32, 32), 0) == lax.broadcasted_iota(jnp.int32, (32, 32), 1)
@@ -208,16 +301,16 @@
         chooser[c * 128:(c + 1) * 128, :] = jnp.where(rows == target, 1.0, 0.0).astype(BF16)
 
     c_old.wait()
-    for c in range(OLD // 32):
-        blk = oldbuf[2 * c:2 * c + 2].reshape(32, 16, HD).astype(F32)
-        head = lax.broadcasted_iota(jnp.int32, (1, 16, 1), 1)
-        for m in range(2):
-            one = jnp.sum(jnp.where(head == 2 * g + m, blk, 0.0), axis=1)
-            oldkv[m, c * 32:(c + 1) * 32, :] = one.astype(BF16)
-
-    pl.semaphore_wait(flood.at[1], 2)
-    signal_round(2)
-
+    pick_row = lax.broadcasted_iota(jnp.int32, (32, 256), 0)
+    pick_col = lax.broadcasted_iota(jnp.int32, (32, 256), 1)
+    wanted = (pick_row % 16) * 16 + 2 * g + pick_row // 16
+    pick = jnp.where(pick_col == wanted, 1.0, 0.0).astype(BF16)
+    for c in range(OLD // 16):
+        both = dot(pick, oldbuf[c].reshape(256, HD)).astype(BF16)
+        oldkv[0, c * 16:(c + 1) * 16, :] = both[:16]
+        oldkv[1, c * 16:(c + 1) * 16, :] = both[16:]
+
+    second_step(0)
     c_tab.wait()
     c_ctx.wait()
     col = lax.broadcasted_iota(jnp.int32, (ROWS, OLD + FRESH), 1)
@@ -243,11 +336,12 @@
             send_sem=aa_s.at[c], recv_sem=aa_r.at[c], device_id=(dst, t), device_id_type=MESH,
         )
 
-    def page_start(c):
+    def page_start(chunks, begin, end):
         def body(i, _):
-            page_copy(c, i).start()
+            for c in chunks:
+                page_copy(c, i).start()
             return 0
-        lax.fori_loop(0, 31, body, 0)
+        lax.fori_loop(begin, end, body, 0)
 
     def pages_all(c):
         most = pl.ds(0, 31 * MSG)
@@ -256,35 +350,20 @@
             send_sem=aa_s.at[c], recv_sem=aa_r.at[c], device_id=sib, device_id_type=MESH,
         )
 
+    second_step(1)
+
     own = pl.ds(pl.multiple_of(s * MSG, MSG), MSG)
-    total_sq = chip_sq
-    scales = {}
     for c in range(2):
-        upper = part[c, g, k, 0:128]
-        lower = part[c, g, k, 128:256]
-        for i in (5, 6, 3, 4, 1, 2, 0):
-            p = c * 8 + i
-            c_sq[p].wait_recv()
-            src = ring_src(i)
-            stat = rstat[c, src]
-            if c == 0:
-                total_sq = total_sq + stat
-                ms = stat * (1.0 / (2 * FEAT)) + TINY
-                scales[i] = (ms * lax.rsqrt(ms)).T
-            col_scale = stat[4:5, :]
-            c_rs[p].wait_recv()
-            got = rs[c, src].astype(jnp.int32).astype(F32) * col_scale
-            upper = upper + got[:128] * scales[i][:, 2 * c:2 * c + 1]
-            lower = lower + got[128:] * scales[i][:, 2 * c + 1:2 * c + 2]
-        if c == 0:
-            inv = lax.rsqrt(total_sq / D + NORM_EPS).T
-        kvc[c, 0:128] = (upper * inv[:, 2 * c:2 * c + 1]).astype(BF16)
-        kvc[c, 128:256] = (lower * inv[:, 2 * c + 1:2 * c + 2]).astype(BF16)
+        last_step(c)
         if c == 0:
             pl.semaphore_wait(flood.at[2], 2)
         for r in range(2):
             outg[c, r * 256:(r + 1) * 256] = dot(chooser[r * 256:(r + 1) * 256, :], kvc[c]).astype(BF16)
-        page_start(c)
+        if c == 0:
+            page_start((0,), 0, EARLY)
+        else:
+            page_start((1,), 0, EARLY)
+            page_start((0, 1), EARLY, 31)
         pool[k, c, own, :] = outg[c, own, :]
     halves = [kvc[c].astype(F32).reshape(TOK // PAGE, HALF, HD) for c in range(2)]
     kvh[k] = jnp.concatenate(halves, axis=1).reshape(TOK, HD).astype(BF16)
@@ -317,7 +396,7 @@
     peak = jnp.max(score[0], axis=-1, keepdims=True)
     half = FRESH // 2
     c_pool = []
-    for c in [c_st] + list(c_ps.values()) + list(c_rs.values()) + list(c_sq.values()):
+    for c in [c_st] + list(c_ps.values()) + sends:
         c.wait_send()
     for c in range(2):
         pages_all(c).wait_recv()
@@ -335,8 +414,7 @@
         mixed = mixed + dot((raised[1 + c] * norm).astype(BF16), pool[1, c])
     mixed = mixed.astype(BF16)
     for n in range(NH):
-        dbuf[:, n * HD:(n + 1) * HD] = mixed[n * ROWS:(n + 1) * ROWS]
-    out_copies.append(load(dbuf, o_dec, out_sem.at[4]))
+        o_dec[:, n * HD:(n + 1) * HD] = mixed[n * ROWS:(n + 1) * ROWS]
 
     for c in [c_kv] + c_pool:
         c.wait_send()
@@ -360,21 +438,21 @@
             jax.ShapeDtypeStruct((ROWS, NH * HD), BF16),
         ),
         in_specs=[any_spec] * 10,
-        out_specs=(any_spec, any_spec),
+        out_specs=(any_spec, pl.BlockSpec(memory_space=vm)),
         scratch_shapes=[
             vm((TOK, FEAT), BF16), vm((FEAT,), BF16), vm((CHIPS, FEAT, 2 * HD), BF16),
             vm((1, TOK), I32), vm((1, 32), I32), vm((ROWS, MAXP), I32), pltpu.SMEM((ROWS,), I32),
             vm((TOK, FEAT), BF16), vm((2, 8, 128), F32),
-            vm((2, CHIPS, 2, CH, HD), F32), vm((2, CHIPS, CH, HD), F32),
-            vm((2, CHIPS, CH, HD), I16), vm((2, CHIPS, CH, HD), I16),
-            vm((2, CHIPS, 8, HD), F32), vm((2, CHIPS, 8, HD), F32),
+            vm((CHIPS, 2, TOK, HD), F32), vm((CHIPS, TOK, HD), F32),
+            vm((CHIPS, TOK, HD), I16), vm((2, 4, RH, HD), I16), vm((2, 14, RH, HD), I16),
+            vm((12, 8, HD), F32), vm((12, 8, HD), F32), vm((TOK, HD), F32),
             vm((FRESH // 2, CH), BF16), vm((2, CH, HD), BF16), vm((2, FRESH // 2, HD), BF16),
             vm((2, TOK, HD), BF16), vm((2, 2, FRESH // 2, HD), BF16),
             vm((16, 16, 16, HD), BF16), vm((2, OLD, HD), BF16), vm((TOK, NH * HD), BF16),
             vm((ROWS, NH * HD), BF16), vm((ROWS, OLD + FRESH), F32),
-            vm((TOK, NH * HD), BF16), vm((ROWS, NH * HD), BF16),
-            dma((9,)), dma((8,)), dma((4,)), dma((4,)), dma((16,)), dma((16,)), dma((2, 7)), dma((2, 7)),
-            dma((2, 7)), dma((2, 7)), dma((2,)), dma((2,)), dma((5,)), pltpu.SemaphoreType.REGULAR((3,)),
+            vm((TOK, NH * HD), BF16),
+            dma((9,)), dma((8,)), dma((4,)), dma((4,)), dma((8,)), dma((8,)), dma((28,)), dma((28,)),
+            dma((12,)), dma((12,)), dma((2,)), dma((2,)), dma((4,)), pltpu.SemaphoreType.REGULAR((3,)),
         ],
         compiler_params=pltpu.CompilerParams(
             collective_id=0, has_side_effects=True, vmem_limit_bytes=VMEM_LIMIT

time: 47.8 us -> 47 us (0.983)
  Pallas kernels: 43.8 us -> 42.9 us
    pallas_call x1, Pallas kernels: 43.8 us -> 42.9 us  [local(): pl.pallas_call(kernel, name='serve', out_shape=(jax.ShapeDtypeStruct((TOK...]
where the time goes in v4:
time: 47 us; the launch traced here: 46.7 us
  Pallas kernels  42.9 us (91%)
  local copies, waits for them, and re-layouts  3.19 us (7%)
  between operations  0.64 us (1%)
    pallas_call x1, Pallas kernels, local(): pl.pallas_call(kernel, name='serve', out_shape=(jax.ShapeDtypeStruct((TOK...  42.9 us
    unnamed x2, local copies, waits for them, and re-layouts  3.19 us

profile of v4, /device:TPU:1, one launch (start us, length us, event | category | flops | bytes accessed | tf_op | source)
XLA Modules:
  0.0 46.7 jit_solution(17059564224994425783)
XLA Ops:
  0.6 42.9 %serve.1 = (bf16[512,512]{1,0:T(8,128)(2,1)}, bf16[16,512]{1,0:T(8,128)(2,1)}) custom-call(bf16[512,512]{1,0:T(8,128)(2,1)} %hid.1, bf16[512]{0:T(512)(128)(2,1)} %gain.1, bf16[512,2048]{1,0:T(8,128)(2,1)} %weight.1, bf16[512,512]{1,0:T(8,128)(2,1)} %qpre.1, s32[1,512]{1,0:T(1,128)} %doc.1, s32[1,32]{1,0:T(1,128)} %bitcast.1, ...), custom_call_target="tpu_custom_call" | custom-call | tf_op jit(solution)/shard_map/serve/pallas_call | solution.py:433
  43.5 1.9 %copy.14 = bf16[512,512]{1,0:T(8,128)(2,1)} copy(bf16[512,512]{1,0:T(8,128)(2,1)} %get-tuple-element.4) | data formatting | bytes 1048576
  45.4 1.3 %copy.15 = bf16[16,512]{1,0:T(8,128)(2,1)} copy(bf16[16,512]{1,0:T(8,128)(2,1)} %get-tuple-element.5) | data formatting | bytes 32768

commit v5 on v4

--- a/solution.py
+++ b/solution.py
@@ -18,8 +18,8 @@
 MSG = SLOTS * HALF
 FRESH = SECT * SLOTS * PAGE
 LAG = 2
-AHEAD = 3
-EARLY = 6
+AHEAD = 2
+EARLY = 10
 RH = CH // 2
 KEYS = ((1, 2), (0, 2), (1, 1), (0, 1), (1, 0), (1, 3), (0, 3), (0, 0))
 ROWS = 16
@@ -401,7 +401,6 @@
     for c in range(2):
         pages_all(c).wait_recv()
         c_pool.append(remote(pool.at[k, c], pool.at[k, c], sib_s.at[2 + c], sib_r.at[2 + c], sib))
-    for c in range(2):
         c_pool[c].wait_recv()
         sc = dot_t(qs, pool[0, c]) * SCALE + mask[:, OLD + c * half:OLD + (c + 1) * half]
         score.append(sc)

time: 47 us -> 46.3 us (0.985)
  Pallas kernels: 42.9 us -> 42.3 us
    pallas_call x1, Pallas kernels: 42.9 us -> 42.3 us  [local(): pl.pallas_call(kernel, name='serve', out_shape=(jax.ShapeDtypeStruct((TOK...]
where the time goes in v5:
time: 46.3 us; the launch traced here: 46.1 us
  Pallas kernels  42.3 us (91%)
  local copies, waits for them, and re-layouts  3.19 us (7%)
  between operations  0.64 us (1%)
    pallas_call x1, Pallas kernels, local(): pl.pallas_call(kernel, name='serve', out_shape=(jax.ShapeDtypeStruct((TOK...  42.3 us
    unnamed x2, local copies, waits for them, and re-layouts  3.19 us

profile of v5, /device:TPU:1, one launch (start us, length us, event | category | flops | bytes accessed | tf_op | source)
XLA Modules:
  0.0 46.1 jit_solution(8609186093151811022)
XLA Ops:
  0.6 42.3 %serve.1 = (bf16[512,512]{1,0:T(8,128)(2,1)}, bf16[16,512]{1,0:T(8,128)(2,1)}) custom-call(bf16[512,512]{1,0:T(8,128)(2,1)} %hid.1, bf16[512]{0:T(512)(128)(2,1)} %gain.1, bf16[512,2048]{1,0:T(8,128)(2,1)} %weight.1, bf16[512,512]{1,0:T(8,128)(2,1)} %qpre.1, s32[1,512]{1,0:T(1,128)} %doc.1, s32[1,32]{1,0:T(1,128)} %bitcast.1, ...), custom_call_target="tpu_custom_call" | custom-call | tf_op jit(solution)/shard_map/serve/pallas_call | solution.py:432
  42.9 1.9 %copy.14 = bf16[512,512]{1,0:T(8,128)(2,1)} copy(bf16[512,512]{1,0:T(8,128)(2,1)} %get-tuple-element.4) | data formatting | bytes 1048576
  44.8 1.3 %copy.15 = bf16[16,512]{1,0:T(8,128)(2,1)} copy(bf16[16,512]{1,0:T(8,128)(2,1)} %get-tuple-element.5) | data formatting | bytes 32768

commit v6 on v5

--- a/solution.py
+++ b/solution.py
@@ -284,6 +284,8 @@
         kvc[c, 0:RH] = (top * spread(known["inv"], 2 * c)).astype(BF16)
         kvc[c, RH:CH] = (low * spread(known["inv"], 2 * c + 1)).astype(BF16)
 
+    second_step(0)
+
     c_pd.wait()
     eye = lax.broadcasted_iota(jnp.int32, (32, 32), 0) == lax.broadcasted_iota(jnp.int32, (32, 32), 1)
     page_col = jnp.sum(jnp.where(eye, jnp.broadcast_to(pdv[...], (32, 32)), 0), axis=1, keepdims=True)
@@ -299,34 +301,6 @@
     for c in range(4):
         rows = lax.broadcasted_iota(jnp.int32, (128, CH), 0) + c * 128
         chooser[c * 128:(c + 1) * 128, :] = jnp.where(rows == target, 1.0, 0.0).astype(BF16)
-
-    c_old.wait()
-    pick_row = lax.broadcasted_iota(jnp.int32, (32, 256), 0)
-    pick_col = lax.broadcasted_iota(jnp.int32, (32, 256), 1)
-    wanted = (pick_row % 16) * 16 + 2 * g + pick_row // 16
-    pick = jnp.where(pick_col == wanted, 1.0, 0.0).astype(BF16)
-    for c in range(OLD // 16):
-        both = dot(pick, oldbuf[c].reshape(256, HD)).astype(BF16)
-        oldkv[0, c * 16:(c + 1) * 16, :] = both[:16]
-        oldkv[1, c * 16:(c + 1) * 16, :] = both[16:]
-
-    second_step(0)
-    c_tab.wait()
-    c_ctx.wait()
-    col = lax.broadcasted_iota(jnp.int32, (ROWS, OLD + FRESH), 1)
-    fresh = col - OLD
-    within = fresh % (FRESH // 2)
-    col_slot = jnp.where(col < OLD, col // PAGE, 16 + within // HALF)
-    col_in = jnp.where(col < OLD, col % PAGE, (fresh // (FRESH // 2)) * HALF + within % HALF)
-    where_pos = jnp.full((ROWS, OLD + FRESH), 1 << 20, jnp.int32)
-    tab = tabv[...]
-    for j in range(MAXP):
-        where_pos = jnp.where(tab[:, j:j + 1] == col_slot, j * PAGE + col_in, where_pos)
-    row_id = lax.broadcasted_iota(jnp.int32, (ROWS, 1), 0)
-    lens = jnp.zeros((ROWS, 1), jnp.int32)
-    for r in range(ROWS):
-        lens = jnp.where(row_id == r, ctxs[r], lens)
-    pos[...] = jnp.where(where_pos < lens, 0.0, NEG)
 
     def page_copy(c, i):
         dst = i + (SECT + i - s) // SECT
@@ -388,6 +362,33 @@
             wts = softmax_weights(jnp.where(allowed, sc, NEG))
             obuf[q0:hi, n * HD:(n + 1) * HD] = dot(wts, values).astype(BF16)
         out_copies.append(load(obuf.at[q0:hi], o_pre.at[q0:hi], out_sem.at[b]))
+
+    c_old.wait()
+    pick_row = lax.broadcasted_iota(jnp.int32, (32, 256), 0)
+    pick_col = lax.broadcasted_iota(jnp.int32, (32, 256), 1)
+    wanted = (pick_row % 16) * 16 + 2 * g + pick_row // 16
+    pick = jnp.where(pick_col == wanted, 1.0, 0.0).astype(BF16)
+    for c in range(OLD // 16):
+        both = dot(pick, oldbuf[c].reshape(256, HD)).astype(BF16)
+        oldkv[0, c * 16:(c + 1) * 16, :] = both[:16]
+        oldkv[1, c * 16:(c + 1) * 16, :] = both[16:]
+
+    c_tab.wait()
+    c_ctx.wait()
+    col = lax.broadcasted_iota(jnp.int32, (ROWS, OLD + FRESH), 1)
+    fresh = col - OLD
+    within = fresh % (FRESH // 2)
+    col_slot = jnp.where(col < OLD, col // PAGE, 16 + within // HALF)
+    col_in = jnp.where(col < OLD, col % PAGE, (fresh // (FRESH // 2)) * HALF + within % HALF)
+    where_pos = jnp.full((ROWS, OLD + FRESH), 1 << 20, jnp.int32)
+    tab = tabv[...]
+    for j in range(MAXP):
+        where_pos = jnp.where(tab[:, j:j + 1] == col_slot, j * PAGE + col_in, where_pos)
+    row_id = lax.broadcasted_iota(jnp.int32, (ROWS, 1), 0)
+    lens = jnp.zeros((ROWS, 1), jnp.int32)
+    for r in range(ROWS):
+        lens = jnp.where(row_id == r, ctxs[r], lens)
+    pos[...] = jnp.where(where_pos < lens, 0.0, NEG)
 
     c_qd.wait()
     qs = jnp.concatenate([qd[:, n * HD:(n + 1) * HD] for n in range(NH)], axis=0)

time: 46.3 us -> 46.8 us (1.011)
  Pallas kernels: 42.3 us -> 42.8 us
    pallas_call x1, Pallas kernels: 42.3 us -> 42.8 us  [local(): pl.pallas_call(kernel, name='serve', out_shape=(jax.ShapeDtypeStruct((TOK...]
where the time goes in v6:
time: 46.8 us; the launch traced here: 46.6 us
  Pallas kernels  42.8 us (91%)
  local copies, waits for them, and re-layouts  3.19 us (7%)
  between operations  0.64 us (1%)
    pallas_call x1, Pallas kernels, local(): pl.pallas_call(kernel, name='serve', out_shape=(jax.ShapeDtypeStruct((TOK...  42.8 us
    unnamed x2, local copies, waits for them, and re-layouts  3.19 us

profile of v6, /device:TPU:1, one launch (start us, length us, event | category | flops | bytes accessed | tf_op | source)
XLA Modules:
  0.0 46.6 jit_solution(11091810509329342504)
XLA Ops:
  0.6 42.8 %serve.1 = (bf16[512,512]{1,0:T(8,128)(2,1)}, bf16[16,512]{1,0:T(8,128)(2,1)}) custom-call(bf16[512,512]{1,0:T(8,128)(2,1)} %hid.1, bf16[512]{0:T(512)(128)(2,1)} %gain.1, bf16[512,2048]{1,0:T(8,128)(2,1)} %weight.1, bf16[512,512]{1,0:T(8,128)(2,1)} %qpre.1, s32[1,512]{1,0:T(1,128)} %doc.1, s32[1,32]{1,0:T(1,128)} %bitcast.1, ...), custom_call_target="tpu_custom_call" | custom-call | tf_op jit(solution)/shard_map/serve/pallas_call | solution.py:433
  43.4 1.9 %copy.14 = bf16[512,512]{1,0:T(8,128)(2,1)} copy(bf16[512,512]{1,0:T(8,128)(2,1)} %get-tuple-element.4) | data formatting | bytes 1048576
  45.3 1.3 %copy.15 = bf16[16,512]{1,0:T(8,128)(2,1)} copy(bf16[16,512]{1,0:T(8,128)(2,1)} %get-tuple-element.5) | data formatting | bytes 32768
